TPU v7x, 32 devices: a whole 2x2x4 slice. The times are simulated.
32 devices in a mesh: groups: 2 (over x), dp: 16 (over z, y, core).
Axes of the slice: x: 2, y: 2, z: 4, core: 2. Of those that a mesh axis runs over, the one named last changes fastest.
Arguments:
- tokens: bfloat16 [16384, 1024], P(('groups', 'dp')), parts along dimension 0, may hold values from -8 to 8
- lengths: int32 [32, 8], P(('groups', 'dp')), parts along dimension 0, may hold values from 1 to 256, 512 in all within a row
- input_weight: bfloat16 [1024, 3072], P(None, 'dp'), may hold values from -0.5 to 0.5
- output_weight: bfloat16 [1024, 1024], P(None, 'dp'), may hold values from -0.1875 to 0.1875
- norm_gain: float32 [1024], replicated, may hold values from 0.25 to 1.75
- expand_weight: bfloat16 [1024, 2048], P(None, 'dp'), may hold values from -0.1875 to 0.1875
- shrink_weight: bfloat16 [2048, 1024], P(None, 'dp'), may hold values from -0.125 to 0.125
- assigned: int32 [16384], P(('groups', 'dp')), parts along dimension 0, may hold values from 0 to 63, as said below
- owner_map: int32 [128], P('groups'), parts along dimension 0, may hold values from 0 to 63, each once
- centroids: bfloat16 [64, 1024], P('dp'), may hold values from -3 to 3
Outputs:
- filed: bfloat16 [128, 256, 1024], P(('groups', 'dp')), parts along dimension 0
There are 2 independent parts, one for each index of `groups`. A program takes and returns all parts, laid end to end along the dimension named above; an argument that names none is the same for every part. Nothing has to cross between parts.
Inputs may be any that keep to these rules, and one draw needn't show every extreme that they name: `assigned`: each device's 512 rows name no list more than 16 times, and one list is named exactly 16 times by the rows of every device. The 8 lengths of a device sum to 512; its passages lie end to end in its rows. `owner_map`: A permutation; the list with value p belongs to the device p // 4.
All inputs are finite; a program needn't handle non-finite values.
Results may differ from a plain program's by a relative error of at most 0.015.
Values may be sent and summed in bfloat16 or wider, within the bound.
No kernel may reach another device: no remote copies, remote signals or barrier semaphores. Data moves between devices by JAX's collectives and lax.ppermute only.
A program may use at most 128 MiB of HBM per device.

v0:
```python
import functools
import math

import jax
import jax.numpy as jnp
from jax import lax
from jax.experimental import pallas as pl
from jax.experimental.pallas import tpu as pltpu
from jax.sharding import PartitionSpec as P

HEADS = 16


norm_eps = 1e-06
ridge_term = 0.05


def layer_norm(values, gain_row):
    row_mean = jnp.mean(values, axis=-1, keepdims=True)
    centered = values - row_mean
    row_var = jnp.mean(centered * centered, axis=-1, keepdims=True)
    return centered * lax.rsqrt(row_var + norm_eps) * gain_row


def segment_ids(length_row, row_count):
    boundary = jnp.cumsum(length_row)
    position = jnp.arange(row_count, dtype=jnp.int32)
    return jnp.sum((position[:, None] >= boundary[None, :]).astype(jnp.int32), axis=1)


HEADS_STEP = 2


def attend_kernel(head_dim, column_ref, row_ref, query_ref, key_ref, value_ref, out_ref, bias):
    @pl.when(pl.program_id(0) == 0)
    def _():
        bias[...] = jnp.where(column_ref[...] == row_ref[...], 0.0, -1e30)

    score_scale = math.log2(math.e) / math.sqrt(head_dim)
    for head in range(HEADS_STEP):
        rows = slice(head * head_dim, (head + 1) * head_dim)
        scores = lax.dot_general(
            key_ref[rows, :], query_ref[rows, :], (((0,), (0,)), ((), ())), preferred_element_type=jnp.float32
        )
        scores = scores * score_scale + bias[...]
        weights = jnp.exp2(scores - jnp.max(scores, axis=0, keepdims=True))
        total = jnp.sum(weights, axis=0, keepdims=True)
        mixed = jnp.dot(value_ref[rows, :], weights.astype(jnp.bfloat16), preferred_element_type=jnp.float32)
        out_ref[rows, :] = (mixed * (1.0 / total)).astype(out_ref.dtype)


def attend(projected, segment):
    width, row_count = projected.shape[0] // 3, projected.shape[1]
    head_dim = width // HEADS
    block = (HEADS_STEP * head_dim, row_count)
    steps = HEADS // HEADS_STEP
    return pl.pallas_call(
        functools.partial(attend_kernel, head_dim),
        grid=(steps,),
        out_shape=jax.ShapeDtypeStruct((width, row_count), jnp.bfloat16),
        in_specs=[
            pl.BlockSpec((row_count, 1), lambda i: (0, 0)),
            pl.BlockSpec((1, row_count), lambda i: (0, 0)),
            pl.BlockSpec(block, lambda i: (i, 0)),
            pl.BlockSpec(block, lambda i: (i + steps, 0)),
            pl.BlockSpec(block, lambda i: (i + 2 * steps, 0)),
        ],
        out_specs=pl.BlockSpec(block, lambda i: (i, 0)),
        scratch_shapes=[pltpu.VMEM((row_count, row_count), jnp.float32)],
        compiler_params=pltpu.CompilerParams(vmem_limit_bytes=32 * 1024 * 1024),
        cost_estimate=pl.CostEstimate(
            flops=4 * HEADS * row_count * row_count * head_dim,
            bytes_accessed=8 * width * row_count,
            transcendentals=HEADS * row_count * row_count,
        ),
    )(segment[:, None], segment[None, :], projected, projected, projected)


def exchange(part, axis, bit):
    return lax.ppermute(part, axis, [(i, i ^ bit) for i in range(lax.axis_size(axis))])


def ordered(part, axis, bit, *beside):
    other = after(exchange(part, axis, bit), *beside)
    low = (lax.axis_index(axis) // bit) % 2 == 0
    return jnp.stack([jnp.where(low, part, other), jnp.where(low, other, part)])


def bits_of(size, least):
    bits = []
    while size // 2 >= least:
        size //= 2
        bits.append(size)
    return bits


def after(part, *earlier):
    return lax.optimization_barrier((part, *earlier))[0] if earlier else part


def own_share(shard):
    groups = lax.axis_size("groups")
    rows, width = shard.shape
    shares = shard.reshape(groups, 2, rows // groups // 2, width)
    return lax.dynamic_index_in_dim(shares, lax.axis_index("groups"), 0, False)


def gather_far(part, bits):
    tail = part.shape[-3:]
    for bit in bits:
        part = ordered(part, "dp", bit)
    return part.reshape((-1,) + tail)


def near_first(part, *beside):
    group_bit = bits_of(lax.axis_size("groups"), 1)[0]
    return ordered(part[:, 0], "dp", 2, *beside), ordered(part[:, 1], "groups", group_bit, *beside)


def near_rest(one, two, *beside):
    group_bits = bits_of(lax.axis_size("groups"), 1)
    for bit in group_bits:
        one = ordered(one, "groups", bit, *beside)
    for bit in group_bits[1:]:
        two = ordered(two, "groups", bit)
    return one, jnp.moveaxis(ordered(two, "dp", 2, *beside), 0, len(group_bits))


def gather_cores(one, two):
    unit, width = one.shape[-2:]
    count, groups = lax.axis_size("dp"), lax.axis_size("groups")
    far_bits, group_bits = len(bits_of(count, 4)), len(bits_of(groups, 1))
    whole = jnp.stack([ordered(one, "dp", 1), ordered(two, "dp", 1)])
    whole = whole.reshape((2,) * (3 + group_bits + far_bits) + (unit, width))
    chip = 2 + group_bits
    order = list(range(chip + far_bits, chip, -1)) + [chip, 1] + list(range(chip - 1, 1, -1)) + [0]
    whole = whole.transpose(order + [chip + far_bits + 1, chip + far_bits + 2])
    return whole.reshape(count * groups * 2 * unit, width)


BLOCK = 128
PANEL = 8


def split_bf16(value):
    high = value.astype(jnp.bfloat16)
    return high, (value - high.astype(jnp.float32)).astype(jnp.bfloat16)


def dot3(left, right, dims):
    lh, ll = left
    rh, rl = right
    dot = functools.partial(lax.dot_general, dimension_numbers=(dims, ((), ())), preferred_element_type=jnp.float32)
    return dot(lh, rh) + (dot(lh, rl) + dot(ll, rh))


def diagonal_inverse(rows):
    count = len(rows)
    lane = lax.broadcasted_iota(jnp.int32, (PANEL, BLOCK), 1)
    sub = lax.broadcasted_iota(jnp.int32, (PANEL, BLOCK), 0)
    shape = (PANEL, BLOCK)
    rows = list(rows)
    result = []
    for p in range(count):
        first = PANEL * p
        panel = rows[p]
        inside = (lane >= first) & (lane < first + PANEL)
        spread = [jnp.broadcast_to(panel[:, first + t : first + t + 1], shape) for t in range(PANEL)]
        entry = [[jnp.broadcast_to(spread[b][a : a + 1, :], shape) for b in range(a + 1)] for a in range(PANEL)]
        columns = [
            [jnp.broadcast_to(rows[i][:, first + t : first + t + 1], shape) for t in range(PANEL)]
            for i in range(p + 1, count)
        ]
        forward = [
            jnp.where(inside, jnp.where(lane == first + t, 1.0, 0.0), jnp.broadcast_to(panel[t : t + 1, :], shape))
            for t in range(PANEL)
        ]
        ratio = [[None] * PANEL for _ in range(PANEL)]
        kept = jnp.zeros(shape, jnp.float32)
        solved = [None] * PANEL
        for t in range(PANEL):
            root = lax.rsqrt(entry[t][t])
            inverse = root * root
            for a in range(t + 1, PANEL):
                ratio[a][t] = entry[a][t] * inverse
            for a in range(t + 1, PANEL):
                for b in range(t + 1, a + 1):
                    entry[a][b] = entry[a][b] - ratio[a][t] * entry[b][t]
            kept = jnp.where(sub == t, forward[t] * root, kept)
            solved[t] = forward[t] * inverse
            for a in range(t + 1, PANEL):
                forward[a] = forward[a] - ratio[a][t] * forward[t]
        for t in range(PANEL - 1, 0, -1):
            for a in range(t):
                solved[a] = solved[a] - ratio[t][a] * solved[t]
        result.append(jnp.where(lane <= first + sub, kept, 0.0))
        for i in range(p + 1, count):
            col = columns[i - p - 1]
            terms = [col[t] * solved[t] for t in range(PANEL)]
            while len(terms) > 1:
                terms = [a + b for a, b in zip(terms[::2], terms[1::2])]
            rows[i] = jnp.where(inside, 0.0, rows[i]) - terms[0]
    return result


def factor_step(work, j):
    blocks = work.shape[0] // BLOCK
    at = slice(j * BLOCK, (j + 1) * BLOCK)
    diagonal = work[at, at]
    inverse = jnp.concatenate(
        diagonal_inverse([diagonal[PANEL * i : PANEL * (i + 1), :] for i in range(BLOCK // PANEL)]), axis=0
    )
    pair = split_bf16(inverse)
    work[at, at] = identity(BLOCK)
    scaled = dot3(pair, split_bf16(work[at, :]), ((1,), (0,)))
    work[at, :] = scaled
    if j + 1 == blocks:
        return
    scaled_pair = split_bf16(scaled)
    below = slice((j + 1) * BLOCK, blocks * BLOCK)
    left = dot3(split_bf16(work[below, at]), pair, ((1,), (1,)))
    work[below, at] = jnp.zeros((left.shape[0], BLOCK), jnp.float32)
    work[below, :] = work[below, :] - dot3(split_bf16(left), scaled_pair, ((1,), (0,)))


def factor_in_place(work):
    for j in range(work.shape[0] // BLOCK):
        factor_step(work, j)


def identity(size):
    return (
        lax.broadcasted_iota(jnp.int32, (size, size), 0) == lax.broadcasted_iota(jnp.int32, (size, size), 1)
    ).astype(jnp.float32)


def block_lower(value):
    row = lax.broadcasted_iota(jnp.int32, value.shape, 0) // BLOCK
    column = lax.broadcasted_iota(jnp.int32, value.shape, 1) // BLOCK
    return jnp.where(column <= row, value, 0.0)


def load_symmetric(tiles, scale, ridge, work):
    side = tiles[0].shape[0]
    diagonal = ridge * identity(side)
    low, high = slice(0, side), slice(side, 2 * side)
    work[low, low] = tiles[0][...] * scale + diagonal
    work[high, high] = tiles[1][...] * scale + diagonal
    cross = tiles[2][...] * scale
    work[high, low] = cross
    work[low, high] = cross.T


def first_kernel(scale, ridge, tiles_ref, out_ref):
    load_symmetric([tiles_ref.at[i] for i in range(3)], scale, ridge, out_ref)
    factor_step(out_ref, 0)


def later_kernel(j, work_ref, out_ref):
    out_ref[...] = work_ref[...]
    factor_step(out_ref, j)
    if (j + 1) * BLOCK == out_ref.shape[0]:
        out_ref[...] = block_lower(out_ref[...])


def second_kernel(scale, ridge, first_ref, tiles_ref, out_ref, work, under):
    half = first_ref.shape[0]
    side = half // 2
    load_symmetric([tiles_ref.at[4 + i] for i in range(3)], scale, ridge, work)
    first = split_bf16(first_ref[...])
    for i in range(2):
        rows = slice(i * side, (i + 1) * side)
        cross = jnp.concatenate([tiles_ref[2 * i], tiles_ref[2 * i + 1]], axis=1) * scale
        under[rows, :] = dot3(split_bf16(cross), first, ((1,), (1,)))
    pair = split_bf16(under[...])
    for i in range(2):
        rows = slice(i * side, (i + 1) * side)
        mine = tuple(part[rows, :] for part in pair)
        work[rows, :] = work[rows, :] - dot3(mine, pair, ((1,), (1,)))
    under[...] = dot3(pair, first, ((1,), (0,)))
    factor_in_place(work)
    second = block_lower(work[...])
    out_ref[:half, :half] = first_ref[...].astype(out_ref.dtype)
    out_ref[:half, half:] = jnp.zeros((half, half), out_ref.dtype)
    out_ref[half:, :half] = (-dot3(split_bf16(second), split_bf16(under[...]), ((1,), (0,)))).astype(out_ref.dtype)
    out_ref[half:, half:] = second.astype(out_ref.dtype)


def kernel_call(kernel, out, operands, scratch, cost):
    whole = pl.BlockSpec(memory_space=pltpu.VMEM)
    return pl.pallas_call(
        kernel,
        out_shape=out,
        in_specs=[whole] * len(operands),
        out_specs=whole,
        scratch_shapes=scratch,
        compiler_params=pltpu.CompilerParams(vmem_limit_bytes=40 * 1024 * 1024),
        cost_estimate=pl.CostEstimate(flops=cost, bytes_accessed=4 << 20, transcendentals=0),
    )(*operands)


CHAIN_FLOPS = 30_000_000_000


def inverse_first(tiles, scale, ridge):
    half = 2 * tiles.shape[-1]
    shape = jax.ShapeDtypeStruct((half, half), jnp.float32)
    steps = half // BLOCK
    stages = [
        kernel_call(functools.partial(first_kernel, scale, ridge), shape, (tiles,), [], CHAIN_FLOPS // steps)
    ]
    for j in range(1, steps):
        stages.append(
            kernel_call(functools.partial(later_kernel, j), shape, (stages[-1],), [], CHAIN_FLOPS // steps)
        )
    return stages


def inverse_second(first, tiles, scale, ridge):
    half = first.shape[0]
    square = pltpu.VMEM((half, half), jnp.float32)
    return kernel_call(
        functools.partial(second_kernel, scale, ridge),
        jax.ShapeDtypeStruct((2 * half, 2 * half), jnp.bfloat16),
        (first, tiles),
        [square, square],
        CHAIN_FLOPS,
    )


FIRST_TILES = ((0, 0), (1, 1), (1, 0))
SECOND_TILES = ((2, 0), (2, 1), (3, 0), (3, 1), (2, 2), (3, 3), (3, 2))


def gram_kernel(rows_ref, columns_ref, left_ref, right_ref, out_ref):
    out_ref[0] = lax.dot_general(
        left_ref[...], right_ref[...], (((0,), (0,)), ((), ())), preferred_element_type=jnp.float32
    )


def gram_tiles(values, tiles):
    count, width = values.shape
    side = width // 4
    rows = jnp.array([tile[0] for tile in tiles], jnp.int32)
    columns = jnp.array([tile[1] for tile in tiles], jnp.int32)
    return pl.pallas_call(
        gram_kernel,
        grid_spec=pltpu.PrefetchScalarGridSpec(
            num_scalar_prefetch=2,
            grid=(len(tiles),),
            in_specs=[
                pl.BlockSpec((count, side), lambda i, row, column: (0, row[i])),
                pl.BlockSpec((count, side), lambda i, row, column: (0, column[i])),
            ],
            out_specs=pl.BlockSpec((1, side, side), lambda i, row, column: (i, 0, 0)),
        ),
        out_shape=jax.ShapeDtypeStruct((len(tiles), side, side), jnp.float32),
        compiler_params=pltpu.CompilerParams(vmem_limit_bytes=24 * 1024 * 1024),
        cost_estimate=pl.CostEstimate(
            flops=2 * len(tiles) * count * side * side, bytes_accessed=4 << 20, transcendentals=0
        ),
    )(rows, columns, values, values)


def halve(part, bit, start=(), beside=()):
    halves = part.reshape(2, -1, part.shape[-1])
    high = (lax.axis_index("dp") // bit) % 2
    kept = lax.dynamic_index_in_dim(halves, high, 0, False)
    sent = after(lax.dynamic_index_in_dim(halves, 1 - high, 0, False), *start)
    return kept + after(exchange(sent, "dp", bit), *beside)


def rejoin(part, bit, *beside):
    return ordered(part, "dp", bit, *beside).reshape(-1, part.shape[-1])


def sum_first(part):
    bits = bits_of(lax.axis_size("dp"), 1)[::-1]
    stages = [part]
    for bit in bits[:-2]:
        stages.append(halve(stages[-1], bit))
    for bit in bits[-2:]:
        stages.append(stages[-1] + exchange(stages[-1], "dp", bit))
    for bit in bits[:-2][::-1]:
        stages.append(rejoin(stages[-1], bit))
    return stages[1:]


def sum_second(part, sums, factors):
    bits = bits_of(lax.axis_size("dp"), 1)[::-1]
    gaps = [sums[k + (k >= len(bits) - 2)] for k in range(len(bits))] + [factors[0]]
    for k, bit in enumerate(bits):
        part = halve(part, bit, (gaps[k],), (gaps[k + 1],))
    for k, bit in enumerate(bits[::-1]):
        if bit == 2:
            near = part
        part = rejoin(part, bit, factors[min(k + 1, len(factors) - 1)])
    return part, near


def filing_kernel(rows_ref, inverse_ref, centroids_ref, out_ref):
    count, _, slots, width = rows_ref.shape
    rows = rows_ref[...].reshape(count * slots, width)
    whitened = lax.dot_general(rows, inverse_ref[...], (((1,), (1,)), ((), ())), preferred_element_type=jnp.float32)
    residual = whitened - centroids_ref[0].astype(jnp.float32)
    out_ref[0] = jnp.where(rows[:, :1].astype(jnp.float32) < EMPTY, residual, 0.0).astype(out_ref.dtype)


def file_rows(incoming, inverse, centroids):
    count, lists, slots, width = incoming.shape
    return pl.pallas_call(
        filing_kernel,
        grid=(lists,),
        in_specs=[
            pl.BlockSpec((count, 1, slots, width), lambda i: (0, i, 0, 0)),
            pl.BlockSpec((width, width), lambda i: (0, 0)),
            pl.BlockSpec((1, 1, width), lambda i: (i, 0, 0)),
        ],
        out_specs=pl.BlockSpec((1, count * slots, width), lambda i: (i, 0, 0)),
        out_shape=jax.ShapeDtypeStruct((lists, count * slots, width), jnp.bfloat16),
        compiler_params=pltpu.CompilerParams(vmem_limit_bytes=24 * 1024 * 1024),
    )(incoming, inverse, centroids[:, None, :])


EMPTY = 64.0


def slots_of(assigned, owner_map, lists_owned, slot_count):
    row_count = assigned.shape[0]
    choose = assigned[:, None] == jnp.arange(owner_map.shape[0], dtype=jnp.int32)[None, :]
    position = jnp.sum(jnp.where(choose, owner_map[None, :], 0), axis=1)
    order = jnp.arange(row_count, dtype=jnp.int32)
    earlier = (assigned[:, None] == assigned[None, :]) & (order[:, None] > order[None, :])
    rank = jnp.sum(earlier.astype(jnp.int32), axis=1)
    return position * slot_count + rank


def place_rows(rows, slot_index, slot_total):
    chosen = jnp.arange(slot_total, dtype=jnp.int32)[:, None] == slot_index[None, :]
    placed = jnp.dot(chosen.astype(jnp.bfloat16), rows, preferred_element_type=jnp.float32)
    return jnp.where(jnp.any(chosen, axis=1, keepdims=True), placed, EMPTY).astype(jnp.bfloat16)


def body(
    tokens,
    lengths,
    input_weight,
    output_weight,
    norm_gain,
    expand_weight,
    shrink_weight,
    assigned,
    owner_map,
    centroids,
):
    row_count, model_width = tokens.shape
    device_count = lax.axis_size("dp")
    nt = functools.partial(
        lax.dot_general, dimension_numbers=(((1,), (1,)), ((), ())), preferred_element_type=jnp.float32
    )
    middle = jnp.concatenate([output_weight.T, expand_weight.T], axis=0)
    far_bits = bits_of(device_count, 4)
    near, far = far_bits[1:], far_bits[:1]
    input_part = gather_far(gather_far(own_share(input_weight.T), far), near)
    middle_part = gather_far(after(own_share(middle), input_part), far)
    input_part = near_first(input_part)
    middle_part = gather_far(after(middle_part, *input_part), near)
    input_part = near_rest(*input_part)
    shrink_part = gather_far(after(own_share(shrink_weight.T), *input_part), far)
    middle_part = near_first(after(middle_part, *input_part))
    projected = nt(gather_cores(*input_part), tokens).astype(jnp.bfloat16)
    shrink_part = gather_far(after(shrink_part, *middle_part), near)
    attended = attend(after(projected, *middle_part), segment_ids(lengths[0], row_count))
    middle_part = near_rest(*middle_part, attended)
    middle_rows = gather_cores(*middle_part).reshape(device_count, -1, model_width)
    own_output = output_weight.shape[1]
    output_rows = middle_rows[:, :own_output].reshape(-1, model_width)
    expand_rows = middle_rows[:, own_output:].reshape(-1, model_width)
    mixed_out = lax.dot_general(
        attended, output_rows, (((0,), (1,)), ((), ())), preferred_element_type=jnp.float32
    )
    first_norm = layer_norm(tokens.astype(jnp.float32) + mixed_out, norm_gain).astype(jnp.bfloat16)
    shrink_part = near_first(after(shrink_part, *middle_part), first_norm)
    expanded = jax.nn.gelu(nt(after(first_norm, *shrink_part), expand_rows), approximate=False).astype(jnp.bfloat16)
    shrink_part = near_rest(*shrink_part, expanded)
    shrink_rows = gather_cores(*shrink_part)
    reduced = nt(expanded, shrink_rows)
    embedded = layer_norm(first_norm.astype(jnp.float32) + reduced, 1.0).astype(jnp.bfloat16)
    lists_owned = centroids.shape[0]
    list_total = lists_owned * device_count
    slot_count = max(2, 2 * row_count // list_total)
    slot_index = slots_of(assigned, owner_map, lists_owned, slot_count)
    outgoing = place_rows(embedded, slot_index, list_total * slot_count)
    scale = 1.0 / (row_count * device_count)
    first_tiles = gram_tiles(embedded, FIRST_TILES)
    second_tiles = gram_tiles(after(embedded, first_tiles), SECOND_TILES)
    sums = sum_first(first_tiles.reshape(-1, first_tiles.shape[-1]))
    stages = inverse_first(sums[-1].reshape(first_tiles.shape), scale, ridge_term)
    second_sum, near = sum_second(second_tiles.reshape(-1, second_tiles.shape[-1]), sums, stages)
    second_sum = second_sum.reshape(second_tiles.shape)
    first = stages[-1]
    outgoing = after(outgoing, near)
    incoming = lax.all_to_all(
        outgoing.reshape(device_count, lists_owned, slot_count, model_width),
        "dp",
        split_axis=0,
        concat_axis=0,
        tiled=True,
    )
    inverse = inverse_second(first, second_sum, scale, ridge_term)
    if slot_count % 16 == 0:
        return file_rows(incoming, inverse, centroids)
    arrived = incoming.transpose(1, 0, 2, 3).reshape(-1, model_width)
    whitened = lax.dot_general(
        arrived, inverse, (((1,), (1,)), ((), ())), preferred_element_type=jnp.float32
    ).reshape(lists_owned, device_count * slot_count, model_width)
    occupied = arrived[:, :1].reshape(lists_owned, device_count * slot_count, 1) < EMPTY
    residual = whitened - centroids.astype(jnp.float32)[:, None, :]
    return jnp.where(occupied, residual, 0.0).astype(jnp.bfloat16)


def solution(mesh):
    in_specs = (
        P(("groups", "dp"), None),
        P(("groups", "dp"), None),
        P(None, "dp"),
        P(None, "dp"),
        P(),
        P(None, "dp"),
        P(None, "dp"),
        P(("groups", "dp")),
        P("groups"),
        P("dp", None),
    )
    out_specs = P(("groups", "dp"), None, None)
    return jax.shard_map(body, mesh=mesh, in_specs=in_specs, out_specs=out_specs, check_vma=False)
```

profile of v0, /device:TPU:13, one launch (start us, length us, event | category | flops | bytes accessed | tf_op | source)
XLA Modules:
  0.0 288.7 jit_solution(3712557373551543499)
XLA Ops:
  1.0 2.4 collective-permute-start
  3.4 8.7 %collective-permute-done = bf16[2,48,1024]{2,1,0:T(8,128)(2,1)S(1)} collective-permute-done((bf16[2,48,1024]{2,1,0:T(8,128)(2,1)S(1)}, bf16[2,48,1024]{2,1,0:T(8,128)(2,1)S(1)}, u32[]{:S(2)}, u32[]{:S(2)}) %collective-permute-start) | collective-permute-done | bytes 196640 | tf_op jit(solution)/shard_map/ppermute | solution.py:80
  15.3 8.1 %collective-permute-done.1 = bf16[2,2,48,1024]{3,2,1,0:T(8,128)(2,1)S(1)} collective-permute-done((bf16[2,2,48,1024]{3,2,1,0:T(8,128)(2,1)S(1)}, bf16[2,2,48,1024]{3,2,1,0:T(8,128)(2,1)S(1)}, u32[]{:S(2)}, u32[]{:S(2)}) %collective-permute-start.1) | collective-permute-done | bytes 393248 | tf_op jit(solution)/shard_map/ppermute | solution.py:80
  23.5 3.2 %collective-permute-start.8 = (bf16[2,48,1024]{2,1,0:T(8,128)(2,1)S(1)}, bf16[2,48,1024]{2,1,0:T(8,128)(2,1)S(1)}, u32[]{:S(2)}, u32[]{:S(2)}) collective-permute-start(bf16[2,48,1024]{2,1,0:T(8,128)(2,1)S(1)} %dynamic-slice_bitcast_fusion.5), channel_id=1, source_target_pairs={{0,8},{1,9},{2,10},{3,11},{4,12},{5,13},{6,14},{7,15},{8,0},{9,1},... | collective-permute-start | bytes 589832 | tf_op jit(solution)/shard_map/ppermute | solution.py:80
  28.2 7.2 %collective-permute-done.8 = bf16[2,48,1024]{2,1,0:T(8,128)(2,1)S(1)} collective-permute-done((bf16[2,48,1024]{2,1,0:T(8,128)(2,1)S(1)}, bf16[2,48,1024]{2,1,0:T(8,128)(2,1)S(1)}, u32[]{:S(2)}, u32[]{:S(2)}) %collective-permute-start.8) | collective-permute-done | bytes 196640 | tf_op jit(solution)/shard_map/ppermute | solution.py:80
  42.5 4.4 %collective-permute-done.9 = bf16[2,2,48,1024]{3,2,1,0:T(8,128)(2,1)S(1)} collective-permute-done((bf16[2,2,48,1024]{3,2,1,0:T(8,128)(2,1)S(1)}, bf16[2,2,48,1024]{3,2,1,0:T(8,128)(2,1)S(1)}, u32[]{:S(2)}, u32[]{:S(2)}) %collective-permute-start.9) | collective-permute-done | bytes 393248 | tf_op jit(solution)/shard_map/ppermute | solution.py:80
  47.0 9.2 %collective-permute-done.3 = bf16[2,4,48,1024]{3,2,1,0:T(8,128)(2,1)} collective-permute-done((bf16[2,4,48,1024]{3,2,1,0:T(8,128)(2,1)}, bf16[2,4,48,1024]{3,2,1,0:T(8,128)(2,1)}, u32[]{:S(2)}, u32[]{:S(2)}) %collective-permute-start.3) | collective-permute-done | bytes 786464 | tf_op jit(solution)/shard_map/ppermute | solution.py:80
  57.6 3.7 %collective-permute-start.4 = (bf16[2,2,4,48,1024]{4,3,2,1,0:T(8,128)(2,1)S(1)}, bf16[2,2,4,48,1024]{4,3,2,1,0:T(8,128)(2,1)S(1)}, u32[]{:S(2)}, u32[]{:S(2)}) collective-permute-start(bf16[2,2,4,48,1024]{4,3,2,1,0:T(8,128)(2,1)S(1)} %pad_maximum_fusion.1), channel_id=1, source_target_pairs={{0,1},{1,0},{2,3},{3,2},{4,5},{5,4},{6,7},{7,6},{8,9},{9,8},{10,11... | collective-permute-start | bytes 4718600 | tf_op jit(solution)/shard_map/ppermute | solution.py:80
  61.8 2.1 collective-permute-start.16
  65.5 3.7 %collective-permute-done.16 = bf16[2,16,2048]{2,1,0:T(8,128)(2,1)S(1)} collective-permute-done((bf16[2,16,2048]{2,1,0:T(8,128)(2,1)S(1)}, bf16[2,16,2048]{2,1,0:T(8,128)(2,1)S(1)}, u32[]{:S(2)}, u32[]{:S(2)}) %collective-permute-start.16) | collective-permute-done | bytes 131104 | tf_op jit(solution)/shard_map/ppermute | solution.py:80
  69.2 4.9 %collective-permute-done.11 = bf16[4,48,1024]{2,1,0:T(8,128)(2,1)S(1)} collective-permute-done((bf16[4,48,1024]{2,1,0:T(8,128)(2,1)S(1)}, bf16[4,48,1024]{2,1,0:T(8,128)(2,1)S(1)}, u32[]{:S(2)}, u32[]{:S(2)}) %collective-permute-start.11) | collective-permute-done | bytes 393248 | tf_op jit(solution)/shard_map/ppermute | solution.py:80
  76.0 1.5 collective-permute-start.17
  80.5 3.7 %convolution_convert_fusion.query_ref.key_ref.value_ref = bf16[3072,512]{1,0:T(8,128)(2,1)S(1)} fusion(bf16[3072,1024]{1,0:T(8,128)(2,1)S(1)} %bitcast.283, bf16[512,1024]{1,0:T(8,128)(2,1)S(1)} %copy-done.14), kind=kOutput, calls=%fused_computation.3 | convolution fusion | flops 3222798336 | bytes 10485760 | tf_op jit(solution)/shard_map/dot_general | solution.py:471
  84.3 9.1 %shard_map.136 = bf16[1024,512]{1,0:T(8,128)(2,1)S(1)} custom-call(s32[512,1]{1,0:T(8,128)S(1)} %copy.61.column_ref, s32[1,512]{1,0:T(1,128)S(1)} %bitcast.270, bf16[3072,512]{1,0:T(8,128)(2,1)S(1)} %convolution_convert_fusion.query_ref.key_ref.value_ref, bf16[3072,512]{1,0:T(8,128)(2,1)S(1)} %convolution_convert_fusion.query_ref.key_ref.value_ref, ...), custom_call_target="tpu_custom_call" | custom-call | flops 1073741824 | bytes 4194304 | tf_op jit(solution)/shard_map/pallas_call | solution.py:57
  94.9 2.7 collective-permute-start.13
  100.9 2.0 collective-permute-done.15
  106.6 1.4 fusion.13
  110.1 1.3 collective-permute-start.22
  111.4 12.4 %fusion.2 = bf16[512,2048]{1,0:T(8,128)(2,1)} fusion(bf16[512,1024]{1,0:T(8,128)(2,1)S(1)} %multiply_convert_fusion.1, bf16[2048,1024]{1,0:T(8,128)(2,1)S(1)} %bitcast.292), kind=kOutput, calls=%fused_computation.6 | convolution fusion | flops 2215641088 | bytes 7340032 | tf_op jit(solution)/shard_map/dot_general | solution.py:484
  127.1 1.4 collective-permute-done.21
  128.5 1.4 broadcast_select_fusion.11
  130.1 1.4 broadcast_select_fusion.9
  133.5 2.5 fusion.14
  136.7 1.6 shard_map.137
  139.6 3.2 %shard_map.138 = f32[7,256,256]{2,1,0:T(8,128)S(1)} custom-call(s32[7]{0:T(128)S(1)} %copy-done.6, s32[7]{0:T(128)S(1)} %copy-done.7, bf16[512,1024]{1,0:T(8,128)(2,1)S(1)} %multiply_convert_fusion.left_ref.right_ref, bf16[512,1024]{1,0:T(8,128)(2,1)S(1)} %multiply_convert_fusion.left_ref.right_ref), custom_call_target="tpu_custom_call" | custom-call | flops 469762048 | bytes 4194304 | tf_op jit(solution)/shard_map/pallas_call | solution.py:346
  145.5 6.1 %collective-permute-done.26 = f32[192,256]{1,0:T(8,128)} collective-permute-done((f32[192,256]{1,0:T(8,128)S(1)}, f32[192,256]{1,0:T(8,128)}, u32[]{:S(2)}, u32[]{:S(2)}) %collective-permute-start.26) | collective-permute-done | bytes 196640 | tf_op jit(solution)/shard_map/ppermute | solution.py:80
  153.0 4.9 %collective-permute-done.28 = f32[192,256]{1,0:T(8,128)S(1)} collective-permute-done((f32[192,256]{1,0:T(8,128)S(1)}, f32[192,256]{1,0:T(8,128)S(1)}, u32[]{:S(2)}, u32[]{:S(2)}) %collective-permute-start.28) | collective-permute-done | bytes 196640 | tf_op jit(solution)/shard_map/ppermute | solution.py:80
  158.0 8.6 %collective-permute-done.29 = f32[192,256]{1,0:T(8,128)S(1)} collective-permute-done((f32[192,256]{1,0:T(8,128)S(1)}, f32[192,256]{1,0:T(8,128)S(1)}, u32[]{:S(2)}, u32[]{:S(2)}) %collective-permute-start.29) | collective-permute-done | bytes 196640 | tf_op jit(solution)/shard_map/ppermute | solution.py:80
  167.3 2.2 bitcast_add_fusion
  172.5 1.9 collective-permute-start.33
  174.7 7.3 %collective-permute-done.27 = f32[448,256]{1,0:T(8,128)S(1)} collective-permute-done((f32[448,256]{1,0:T(8,128)S(1)}, f32[448,256]{1,0:T(8,128)S(1)}, u32[]{:S(2)}, u32[]{:S(2)}) %collective-permute-start.27) | collective-permute-done | bytes 458784 | tf_op jit(solution)/shard_map/ppermute | solution.py:80
  183.2 1.8 collective-permute-start.30
  185.1 3.3 %collective-permute-done.30 = f32[224,256]{1,0:T(8,128)S(1)} collective-permute-done((f32[224,256]{1,0:T(8,128)S(1)}, f32[224,256]{1,0:T(8,128)S(1)}, u32[]{:S(2)}, u32[]{:S(2)}) %collective-permute-start.30) | collective-permute-done | bytes 229408 | tf_op jit(solution)/shard_map/ppermute | solution.py:80
  188.5 3.3 %collective-permute-start.32 = (f32[112,256]{1,0:T(8,128)S(1)}, f32[112,256]{1,0:T(8,128)S(1)}, u32[]{:S(2)}, u32[]{:S(2)}) collective-permute-start(f32[112,256]{1,0:T(8,128)S(1)} %dynamic-slice_bitcast_fusion.8), channel_id=1, source_target_pairs={{0,8},{1,9},{2,10},{3,11},{4,12},{5,13},{6,14},{7,15},{8,0},{9,1},... | collective-permute-start | bytes 344072 | tf_op jit(solution)/shard_map/ppermute | solution.py:80
  191.8 6.7 %shard_map.139.work_ref = f32[512,512]{1,0:T(8,128)S(1)} custom-call(f32[3,256,256]{2,1,0:T(8,128)S(1)} %bitcast.268), custom_call_target="tpu_custom_call" | custom-call | flops 7500000256 | bytes 4194304 | tf_op jit(solution)/shard_map/pallas_call | solution.py:291
  198.6 6.6 %shard_map.140.work_ref = f32[512,512]{1,0:T(8,128)S(1)} custom-call(f32[512,512]{1,0:T(8,128)S(1)} %shard_map.139.work_ref), custom_call_target="tpu_custom_call" | custom-call | flops 7500000256 | bytes 4194304 | tf_op jit(solution)/shard_map/pallas_call | solution.py:291
  205.9 6.9 %shard_map.141.work_ref = f32[512,512]{1,0:T(8,128)S(1)} custom-call(f32[512,512]{1,0:T(8,128)S(1)} %shard_map.140.work_ref), custom_call_target="tpu_custom_call" | custom-call | flops 7500000256 | bytes 4194304 | tf_op jit(solution)/shard_map/pallas_call | solution.py:291
  213.0 5.7 %shard_map.142.first_ref = f32[512,512]{1,0:T(8,128)S(1)} custom-call(f32[512,512]{1,0:T(8,128)S(1)} %shard_map.141.work_ref), custom_call_target="tpu_custom_call" | custom-call | flops 7500000256 | bytes 4194304 | tf_op jit(solution)/shard_map/pallas_call | solution.py:291
  218.7 2.0 collective-permute-done.36
  221.8 5.2 %collective-permute-start.37 = (f32[896,256]{1,0:T(8,128)}, f32[896,256]{1,0:T(8,128)}, u32[]{:S(2)}, u32[]{:S(2)}) collective-permute-start(f32[896,256]{1,0:T(8,128)} %bitcast.119), channel_id=1, source_target_pairs={{0,1},{1,0},{2,3},{3,2},{4,5},{5,4},{6,7},{7,6},{8,9},{9,8},{10,11... | collective-permute-start | bytes 2752520 | tf_op jit(solution)/shard_map/ppermute | solution.py:80
  227.0 2.6 select_convert_fusion
  229.6 6.0 %all-to-all-start = ((bf16[16,4,16,1024]{3,2,1,0:T(8,128)(2,1)}), bf16[16,4,16,1024]{3,2,1,0:T(8,128)(2,1)S(1)}, u32[]{:S(2)}, u32[]{:S(2)}) async-start(bf16[16,4,16,1024]{3,2,1,0:T(8,128)(2,1)} %bitcast.298), calls=%async_computation | async-start | bytes 4194304 | tf_op jit(solution)/shard_map/all_to_all | solution.py:503
  235.7 1.6 select_bitcast_fusion.1
  237.4 28.6 %shard_map.143.inverse_ref = bf16[1024,1024]{1,0:T(8,128)(2,1)S(1)} custom-call(f32[512,512]{1,0:T(8,128)S(1)} %shard_map.142.first_ref, f32[7,256,256]{2,1,0:T(8,128)S(1)} %bitcast.267), custom_call_target="tpu_custom_call" | custom-call | flops 30000001024 | bytes 4194304 | tf_op jit(solution)/shard_map/pallas_call | solution.py:291
  266.0 1.3 copy-done.4
  267.3 15.6 %all-to-all-done.rows_ref = bf16[16,4,16,1024]{3,2,1,0:T(8,128)(2,1)S(1)} async-done(((bf16[16,4,16,1024]{3,2,1,0:T(8,128)(2,1)}), bf16[16,4,16,1024]{3,2,1,0:T(8,128)(2,1)S(1)}, u32[]{:S(2)}, u32[]{:S(2)}) %all-to-all-start) | async-done | bytes 2097184 | tf_op jit(solution)/shard_map/all_to_all | solution.py:503
  282.9 1.6 copy-done.5
  284.5 4.0 %shard_map.144 = bf16[4,256,1024]{2,1,0:T(8,128)(2,1)} custom-call(bf16[16,4,16,1024]{3,2,1,0:T(8,128)(2,1)S(1)} %all-to-all-done.rows_ref, bf16[1024,1024]{1,0:T(8,128)(2,1)S(1)} %copy-done.5, bf16[4,1,1024]{2,1,0:T(2,128)(2,1)S(1)} %copy.73.centroids_ref), custom_call_target="tpu_custom_call" | custom-call | tf_op jit(solution)/shard_map/pallas_call | solution.py:411
  (179 shorter events, 50.8 us)
Async XLA Ops:
  0.0 41.2 %copy-start = (bf16[2048,64]{0,1:T(8,128)(2,1)S(1)}, bf16[2048,64]{0,1:T(8,128)(2,1)}, u32[]{:S(2)}) copy-start(bf16[2048,64]{0,1:T(8,128)(2,1)} %param.20) | copy-start | bytes 786436
  1.0 11.1 %collective-permute-start = (bf16[2,48,1024]{2,1,0:T(8,128)(2,1)S(1)}, bf16[2,48,1024]{2,1,0:T(8,128)(2,1)S(1)}, u32[]{:S(2)}, u32[]{:S(2)}) collective-permute-start(bf16[2,48,1024]{2,1,0:T(8,128)(2,1)S(1)} %dynamic-slice_bitcast_fusion.6), channel_id=1, source_target_pairs={{0,8},{1,9},{2,10},{3,11},{4,12},{5,13},{6,14},{7,15},{8,0},{9,1},... | collective-permute-start | bytes 589832 | tf_op jit(solution)/shard_map/ppermute | solution.py:80
  13.1 10.3 %collective-permute-start.1 = (bf16[2,2,48,1024]{3,2,1,0:T(8,128)(2,1)S(1)}, bf16[2,2,48,1024]{3,2,1,0:T(8,128)(2,1)S(1)}, u32[]{:S(2)}, u32[]{:S(2)}) collective-permute-start(bf16[2,2,48,1024]{3,2,1,0:T(8,128)(2,1)S(1)} %pad_maximum_fusion.16), channel_id=1, source_target_pairs={{0,4},{1,5},{2,6},{3,7},{4,0},{5,1},{6,2},{7,3},{8,12},{9,13},{10,... | collective-permute-start | bytes 1179656 | tf_op jit(solution)/shard_map/ppermute | solution.py:80
  23.5 12.0 %collective-permute-start.8 = (bf16[2,48,1024]{2,1,0:T(8,128)(2,1)S(1)}, bf16[2,48,1024]{2,1,0:T(8,128)(2,1)S(1)}, u32[]{:S(2)}, u32[]{:S(2)}) collective-permute-start(bf16[2,48,1024]{2,1,0:T(8,128)(2,1)S(1)} %dynamic-slice_bitcast_fusion.5), channel_id=1, source_target_pairs={{0,8},{1,9},{2,10},{3,11},{4,12},{5,13},{6,14},{7,15},{8,0},{9,1},... | collective-permute-start | bytes 589832 | tf_op jit(solution)/shard_map/ppermute | solution.py:80
  26.7 14.1 %copy-start.16 = (s32[1,8]{1,0:T(1,128)S(1)}, s32[1,8]{1,0:T(1,128)}, u32[]{:S(2)}) copy-start(s32[1,8]{1,0:T(1,128)} %param.15) | copy-start | bytes 100
  26.7 9.2 %collective-permute-start.2 = (bf16[4,48,1024]{2,1,0:T(8,128)(2,1)S(1)}, bf16[4,48,1024]{2,1,0:T(8,128)(2,1)S(1)}, u32[]{:S(2)}, u32[]{:S(2)}) collective-permute-start(bf16[4,48,1024]{2,1,0:T(8,128)(2,1)S(1)} %get-tuple-element.107), channel_id=1, source_target_pairs={{0,2},{1,3},{2,0},{3,1},{4,6},{5,7},{6,4},{7,5},{8,10},{9,11},{10,... | collective-permute-start | bytes 1179656 | tf_op jit(solution)/shard_map/ppermute | solution.py:80
  27.0 8.9 %collective-permute-start.5 = (bf16[4,48,1024]{2,1,0:T(8,128)(2,1)S(1)}, bf16[4,48,1024]{2,1,0:T(8,128)(2,1)}, u32[]{:S(2)}, u32[]{:S(2)}) collective-permute-start(bf16[4,48,1024]{2,1,0:T(8,128)(2,1)S(1)} %get-tuple-element.108), channel_id=1, source_target_pairs={{0,16},{16,0},{1,17},{17,1},{2,18},{18,2},{3,19},{19,3},{4,20},{20... | collective-permute-start | bytes 1179656 | tf_op jit(solution)/shard_map/ppermute | solution.py:80
  38.9 7.9 %collective-permute-start.9 = (bf16[2,2,48,1024]{3,2,1,0:T(8,128)(2,1)S(1)}, bf16[2,2,48,1024]{3,2,1,0:T(8,128)(2,1)S(1)}, u32[]{:S(2)}, u32[]{:S(2)}) collective-permute-start(bf16[2,2,48,1024]{3,2,1,0:T(8,128)(2,1)S(1)} %pad_maximum_fusion.18), channel_id=1, source_target_pairs={{0,4},{1,5},{2,6},{3,7},{4,0},{5,1},{6,2},{7,3},{8,12},{9,13},{10,... | collective-permute-start | bytes 1179656 | tf_op jit(solution)/shard_map/ppermute | solution.py:80
  39.6 16.6 %collective-permute-start.3 = (bf16[2,4,48,1024]{3,2,1,0:T(8,128)(2,1)}, bf16[2,4,48,1024]{3,2,1,0:T(8,128)(2,1)}, u32[]{:S(2)}, u32[]{:S(2)}) collective-permute-start(bf16[2,4,48,1024]{3,2,1,0:T(8,128)(2,1)} %pad_maximum_fusion.6), channel_id=1, source_target_pairs={{0,16},{16,0},{1,17},{17,1},{2,18},{18,2},{3,19},{19,3},{4,20},{20... | collective-permute-start | bytes 2359304 | tf_op jit(solution)/shard_map/ppermute | solution.py:80
  41.3 20.1 %collective-permute-start.6 = (bf16[2,4,48,1024]{3,2,1,0:T(8,128)(2,1)}, bf16[2,4,48,1024]{3,2,1,0:T(8,128)(2,1)S(1)}, u32[]{:S(2)}, u32[]{:S(2)}) collective-permute-start(bf16[2,4,48,1024]{3,2,1,0:T(8,128)(2,1)} %pad_maximum_fusion.7), channel_id=1, source_target_pairs={{0,2},{1,3},{2,0},{3,1},{4,6},{5,7},{6,4},{7,5},{8,10},{9,11},{10,... | collective-permute-start | bytes 2359304 | tf_op jit(solution)/shard_map/ppermute | solution.py:80
  57.6 19.8 %collective-permute-start.4 = (bf16[2,2,4,48,1024]{4,3,2,1,0:T(8,128)(2,1)S(1)}, bf16[2,2,4,48,1024]{4,3,2,1,0:T(8,128)(2,1)S(1)}, u32[]{:S(2)}, u32[]{:S(2)}) collective-permute-start(bf16[2,2,4,48,1024]{4,3,2,1,0:T(8,128)(2,1)S(1)} %pad_maximum_fusion.1), channel_id=1, source_target_pairs={{0,1},{1,0},{2,3},{3,2},{4,5},{5,4},{6,7},{7,6},{8,9},{9,8},{10,11... | collective-permute-start | bytes 4718600 | tf_op jit(solution)/shard_map/ppermute | solution.py:80
  61.6 15.8 %collective-permute-start.7 = (bf16[2,2,4,48,1024]{4,3,2,1,0:T(8,128)(2,1)S(1)}, bf16[2,2,4,48,1024]{4,3,2,1,0:T(8,128)(2,1)S(1)}, u32[]{:S(2)}, u32[]{:S(2)}) collective-permute-start(bf16[2,2,4,48,1024]{4,3,2,1,0:T(8,128)(2,1)S(1)} %maximum_bitcast_fusion.1), channel_id=1, source_target_pairs={{0,1},{1,0},{2,3},{3,2},{4,5},{5,4},{6,7},{7,6},{8,9},{9,8},{10,11... | collective-permute-start | bytes 4718600 | tf_op jit(solution)/shard_map/ppermute | solution.py:80
  61.8 7.3 %collective-permute-start.16 = (bf16[2,16,2048]{2,1,0:T(8,128)(2,1)S(1)}, bf16[2,16,2048]{2,1,0:T(8,128)(2,1)S(1)}, u32[]{:S(2)}, u32[]{:S(2)}) collective-permute-start(bf16[2,16,2048]{2,1,0:T(8,128)(2,1)S(1)} %dynamic-slice_bitcast_fusion.7), channel_id=1, source_target_pairs={{0,8},{1,9},{2,10},{3,11},{4,12},{5,13},{6,14},{7,15},{8,0},{9,1},... | collective-permute-start | bytes 393224 | tf_op jit(solution)/shard_map/ppermute | solution.py:80
  64.0 10.1 %collective-permute-start.11 = (bf16[4,48,1024]{2,1,0:T(8,128)(2,1)S(1)}, bf16[4,48,1024]{2,1,0:T(8,128)(2,1)S(1)}, u32[]{:S(2)}, u32[]{:S(2)}) collective-permute-start(bf16[4,48,1024]{2,1,0:T(8,128)(2,1)S(1)} %slice_bitcast_fusion.3), channel_id=1, source_target_pairs={{0,16},{16,0},{1,17},{17,1},{2,18},{18,2},{3,19},{19,3},{4,20},{20... | collective-permute-start | bytes 1179656 | tf_op jit(solution)/shard_map/ppermute | solution.py:80
  65.2 9.7 %collective-permute-start.10 = (bf16[4,48,1024]{2,1,0:T(8,128)(2,1)S(1)}, bf16[4,48,1024]{2,1,0:T(8,128)(2,1)S(1)}, u32[]{:S(2)}, u32[]{:S(2)}) collective-permute-start(bf16[4,48,1024]{2,1,0:T(8,128)(2,1)S(1)} %slice_bitcast_fusion), channel_id=1, source_target_pairs={{0,2},{1,3},{2,0},{3,1},{4,6},{5,7},{6,4},{7,5},{8,10},{9,11},{10,... | collective-permute-start | bytes 1179656 | tf_op jit(solution)/shard_map/ppermute | solution.py:80
  75.2 18.2 %collective-permute-start.12 = (bf16[2,4,48,1024]{3,2,1,0:T(8,128)(2,1)S(1)}, bf16[2,4,48,1024]{3,2,1,0:T(8,128)(2,1)}, u32[]{:S(2)}, u32[]{:S(2)}) collective-permute-start(bf16[2,4,48,1024]{3,2,1,0:T(8,128)(2,1)S(1)} %get-tuple-element.131), channel_id=1, source_target_pairs={{0,16},{16,0},{1,17},{17,1},{2,18},{18,2},{3,19},{19,3},{4,20},{20... | collective-permute-start | bytes 2359304 | tf_op jit(solution)/shard_map/ppermute | solution.py:80
  75.7 18.9 %collective-permute-start.14 = (bf16[2,4,48,1024]{3,2,1,0:T(8,128)(2,1)S(1)}, bf16[2,4,48,1024]{3,2,1,0:T(8,128)(2,1)S(1)}, u32[]{:S(2)}, u32[]{:S(2)}) collective-permute-start(bf16[2,4,48,1024]{3,2,1,0:T(8,128)(2,1)S(1)} %get-tuple-element.132), channel_id=1, source_target_pairs={{0,2},{1,3},{2,0},{3,1},{4,6},{5,7},{6,4},{7,5},{8,10},{9,11},{10,... | collective-permute-start | bytes 2359304 | tf_op jit(solution)/shard_map/ppermute | solution.py:80
  76.0 21.9 %collective-permute-start.17 = (bf16[2,2,16,2048]{3,2,1,0:T(8,128)(2,1)S(1)}, bf16[2,2,16,2048]{3,2,1,0:T(8,128)(2,1)S(1)}, u32[]{:S(2)}, u32[]{:S(2)}) collective-permute-start(bf16[2,2,16,2048]{3,2,1,0:T(8,128)(2,1)S(1)} %pad_maximum_fusion.20), channel_id=1, source_target_pairs={{0,4},{1,5},{2,6},{3,7},{4,0},{5,1},{6,2},{7,3},{8,12},{9,13},{10,... | collective-permute-start | bytes 786440 | tf_op jit(solution)/shard_map/ppermute | solution.py:80
  94.9 5.8 %collective-permute-start.13 = (bf16[2,2,4,48,1024]{4,3,2,0,1:T(8,128)(2,1)S(1)}, bf16[2,2,4,48,1024]{4,3,2,0,1:T(8,128)(2,1)S(1)}, u32[]{:S(2)}, u32[]{:S(2)}) collective-permute-start(bf16[2,2,4,48,1024]{4,3,2,0,1:T(8,128)(2,1)S(1)} %pad_maximum_fusion.2), channel_id=1, source_target_pairs={{0,1},{1,0},{2,3},{3,2},{4,5},{5,4},{6,7},{7,6},{8,9},{9,8},{10,11... | collective-permute-start | bytes 4718600 | tf_op jit(solution)/shard_map/ppermute | solution.py:80
  97.8 5.1 %collective-permute-start.15 = (bf16[2,2,4,48,1024]{4,3,2,0,1:T(8,128)(2,1)S(1)}, bf16[2,2,4,48,1024]{4,3,2,0,1:T(8,128)(2,1)S(1)}, u32[]{:S(2)}, u32[]{:S(2)}) collective-permute-start(bf16[2,2,4,48,1024]{4,3,2,0,1:T(8,128)(2,1)S(1)} %maximum_bitcast_fusion.2), channel_id=1, source_target_pairs={{0,1},{1,0},{2,3},{3,2},{4,5},{5,4},{6,7},{7,6},{8,9},{9,8},{10,11... | collective-permute-start | bytes 4718600 | tf_op jit(solution)/shard_map/ppermute | solution.py:80
  98.0 10.6 %collective-permute-start.19 = (bf16[4,16,2048]{2,1,0:T(8,128)(2,1)S(1)}, bf16[4,16,2048]{2,1,0:T(8,128)(2,1)S(1)}, u32[]{:S(2)}, u32[]{:S(2)}) collective-permute-start(bf16[4,16,2048]{2,1,0:T(8,128)(2,1)S(1)} %slice_bitcast_fusion.5), channel_id=1, source_target_pairs={{0,16},{16,0},{1,17},{17,1},{2,18},{18,2},{3,19},{19,3},{4,20},{20... | collective-permute-start | bytes 786440 | tf_op jit(solution)/shard_map/ppermute | solution.py:80
  99.2 9.5 %collective-permute-start.18 = (bf16[4,16,2048]{2,1,0:T(8,128)(2,1)S(1)}, bf16[4,16,2048]{2,1,0:T(8,128)(2,1)S(1)}, u32[]{:S(2)}, u32[]{:S(2)}) collective-permute-start(bf16[4,16,2048]{2,1,0:T(8,128)(2,1)S(1)} %slice_bitcast_fusion.4), channel_id=1, source_target_pairs={{0,2},{1,3},{2,0},{3,1},{4,6},{5,7},{6,4},{7,5},{8,10},{9,11},{10,... | collective-permute-start | bytes 786440 | tf_op jit(solution)/shard_map/ppermute | solution.py:80
  108.9 14.9 %collective-permute-start.20 = (bf16[2,4,16,2048]{3,2,1,0:T(8,128)(2,1)S(1)}, bf16[2,4,16,2048]{3,2,1,0:T(8,128)(2,1)S(1)}, u32[]{:S(2)}, u32[]{:S(2)}) collective-permute-start(bf16[2,4,16,2048]{3,2,1,0:T(8,128)(2,1)S(1)} %pad_maximum_fusion.13), channel_id=1, source_target_pairs={{0,16},{16,0},{1,17},{17,1},{2,18},{18,2},{3,19},{19,3},{4,20},{20... | collective-permute-start | bytes 1572872 | tf_op jit(solution)/shard_map/ppermute | solution.py:80
  110.1 15.8 %collective-permute-start.22 = (bf16[2,4,16,2048]{3,2,1,0:T(8,128)(2,1)S(1)}, bf16[2,4,16,2048]{3,2,1,0:T(8,128)(2,1)S(1)}, u32[]{:S(2)}, u32[]{:S(2)}) collective-permute-start(bf16[2,4,16,2048]{3,2,1,0:T(8,128)(2,1)S(1)} %pad_maximum_fusion.14), channel_id=1, source_target_pairs={{0,2},{1,3},{2,0},{3,1},{4,6},{5,7},{6,4},{7,5},{8,10},{9,11},{10,... | collective-permute-start | bytes 1572872 | tf_op jit(solution)/shard_map/ppermute | solution.py:80
  124.9 3.6 %collective-permute-start.21 = (bf16[2,2,4,16,2048]{4,3,2,0,1:T(8,128)(2,1)}, bf16[2,2,4,16,2048]{4,3,2,0,1:T(8,128)(2,1)}, u32[]{:S(2)}, u32[]{:S(2)}) collective-permute-start(bf16[2,2,4,16,2048]{4,3,2,0,1:T(8,128)(2,1)} %pad_maximum_fusion.3), channel_id=1, source_target_pairs={{0,1},{1,0},{2,3},{3,2},{4,5},{5,4},{6,7},{7,6},{8,9},{9,8},{10,11... | collective-permute-start | bytes 3145736 | tf_op jit(solution)/shard_map/ppermute | solution.py:80
  127.1 3.0 %collective-permute-start.23 = (bf16[2,2,4,16,2048]{4,3,2,0,1:T(8,128)(2,1)}, bf16[2,2,4,16,2048]{4,3,2,0,1:T(8,128)(2,1)}, u32[]{:S(2)}, u32[]{:S(2)}) collective-permute-start(bf16[2,2,4,16,2048]{4,3,2,0,1:T(8,128)(2,1)} %maximum_bitcast_fusion.3), channel_id=1, source_target_pairs={{0,1},{1,0},{2,3},{3,2},{4,5},{5,4},{6,7},{7,6},{8,9},{9,8},{10,11... | collective-permute-start | bytes 3145736 | tf_op jit(solution)/shard_map/ppermute | solution.py:80
  136.0 3.6 %copy-start.6 = (s32[7]{0:T(128)S(1)}, s32[7]{0:T(128)}, u32[]{:S(2)}) copy-start(s32[7]{0:T(128)} %constant.348.clone.rows_ref) | copy-start | bytes 88
  136.0 3.6 %copy-start.7 = (s32[7]{0:T(128)S(1)}, s32[7]{0:T(128)}, u32[]{:S(2)}) copy-start(s32[7]{0:T(128)} %constant.349.clone.columns_ref) | copy-start | bytes 88
  139.2 13.4 %copy-start.10 = (s32[512]{0:T(512)S(1)}, s32[512]{0:T(512)}, u32[]{:S(2)}) copy-start(s32[512]{0:T(512)} %param.21) | copy-start | bytes 6148
  139.2 13.4 %copy-start.13 = (s32[64]{0:T(128)S(1)}, s32[64]{0:T(128)}, u32[]{:S(2)}) copy-start(s32[64]{0:T(128)} %param.22) | copy-start | bytes 772
  139.3 4.6 %collective-permute-start.24 = (f32[384,256]{1,0:T(8,128)S(1)}, f32[384,256]{1,0:T(8,128)}, u32[]{:S(2)}, u32[]{:S(2)}) collective-permute-start(f32[384,256]{1,0:T(8,128)S(1)} %dynamic-slice_bitcast_fusion.2), channel_id=1, source_target_pairs={{0,1},{1,0},{2,3},{3,2},{4,5},{5,4},{6,7},{7,6},{8,9},{9,8},{10,11... | collective-permute-start | bytes 1179656 | tf_op jit(solution)/shard_map/ppermute | solution.py:80
  139.6 4.2 %copy-start.3 = (f32[3,256,256]{2,1,0:T(8,128)S(1)}, f32[3,256,256]{2,1,0:T(8,128)}, u32[]{:S(2)}) copy-start(f32[3,256,256]{2,1,0:T(8,128)} %copy-done.2) | copy-start | bytes 2359300
  144.9 22.4 %collective-permute-start.25 = (f32[896,256]{1,0:T(8,128)}, f32[896,256]{1,0:T(8,128)}, u32[]{:S(2)}, u32[]{:S(2)}) collective-permute-start(f32[896,256]{1,0:T(8,128)} %dynamic-slice_bitcast_fusion), channel_id=1, source_target_pairs={{0,1},{1,0},{2,3},{3,2},{4,5},{5,4},{6,7},{7,6},{8,9},{9,8},{10,11... | collective-permute-start | bytes 2752520 | tf_op jit(solution)/shard_map/ppermute | solution.py:80
  145.2 6.4 %collective-permute-start.26 = (f32[192,256]{1,0:T(8,128)S(1)}, f32[192,256]{1,0:T(8,128)}, u32[]{:S(2)}, u32[]{:S(2)}) collective-permute-start(f32[192,256]{1,0:T(8,128)S(1)} %dynamic-slice_bitcast_fusion.4), channel_id=1, source_target_pairs={{0,2},{1,3},{2,0},{3,1},{4,6},{5,7},{6,4},{7,5},{8,10},{9,11},{10,... | collective-permute-start | bytes 589832 | tf_op jit(solution)/shard_map/ppermute | solution.py:80
  152.6 5.4 %collective-permute-start.28 = (f32[192,256]{1,0:T(8,128)S(1)}, f32[192,256]{1,0:T(8,128)S(1)}, u32[]{:S(2)}, u32[]{:S(2)}) collective-permute-start(f32[192,256]{1,0:T(8,128)S(1)} %bitcast_add_fusion.4), channel_id=1, source_target_pairs={{0,4},{1,5},{2,6},{3,7},{4,0},{5,1},{6,2},{7,3},{8,12},{9,13},{10,... | collective-permute-start | bytes 589832 | tf_op jit(solution)/shard_map/ppermute | solution.py:80
  158.0 8.7 %collective-permute-start.29 = (f32[192,256]{1,0:T(8,128)S(1)}, f32[192,256]{1,0:T(8,128)S(1)}, u32[]{:S(2)}, u32[]{:S(2)}) collective-permute-start(f32[192,256]{1,0:T(8,128)S(1)} %add.168), channel_id=1, source_target_pairs={{0,8},{1,9},{2,10},{3,11},{4,12},{5,13},{6,14},{7,15},{8,0},{9,1},... | collective-permute-start | bytes 589832 | tf_op jit(solution)/shard_map/ppermute | solution.py:80
  166.7 5.8 %collective-permute-start.31 = (f32[192,256]{1,0:T(8,128)S(1)}, f32[192,256]{1,0:T(8,128)S(1)}, u32[]{:S(2)}, u32[]{:S(2)}) collective-permute-start(f32[192,256]{1,0:T(8,128)S(1)} %add.169), channel_id=1, source_target_pairs={{0,2},{1,3},{2,0},{3,1},{4,6},{5,7},{6,4},{7,5},{8,10},{9,11},{10,... | collective-permute-start | bytes 589832 | tf_op jit(solution)/shard_map/ppermute | solution.py:80
  170.6 11.5 %collective-permute-start.27 = (f32[448,256]{1,0:T(8,128)S(1)}, f32[448,256]{1,0:T(8,128)S(1)}, u32[]{:S(2)}, u32[]{:S(2)}) collective-permute-start(f32[448,256]{1,0:T(8,128)S(1)} %dynamic-slice_bitcast_fusion.1), channel_id=1, source_target_pairs={{0,2},{1,3},{2,0},{3,1},{4,6},{5,7},{6,4},{7,5},{8,10},{9,11},{10,... | collective-permute-start | bytes 1376264 | tf_op jit(solution)/shard_map/ppermute | solution.py:80
  172.5 12.5 %collective-permute-start.33 = (f32[384,256]{1,0:T(8,128)S(1)}, f32[384,256]{1,0:T(8,128)S(1)}, u32[]{:S(2)}, u32[]{:S(2)}) collective-permute-start(f32[384,256]{1,0:T(8,128)S(1)} %bitcast.303), channel_id=1, source_target_pairs={{0,1},{1,0},{2,3},{3,2},{4,5},{5,4},{6,7},{7,6},{8,9},{9,8},{10,11... | collective-permute-start | bytes 1179656 | tf_op jit(solution)/shard_map/ppermute | solution.py:80
  183.2 5.2 %collective-permute-start.30 = (f32[224,256]{1,0:T(8,128)S(1)}, f32[224,256]{1,0:T(8,128)S(1)}, u32[]{:S(2)}, u32[]{:S(2)}) collective-permute-start(f32[224,256]{1,0:T(8,128)S(1)} %dynamic-slice_bitcast_fusion.3), channel_id=1, source_target_pairs={{0,4},{1,5},{2,6},{3,7},{4,0},{5,1},{6,2},{7,3},{8,12},{9,13},{10,... | collective-permute-start | bytes 688136 | tf_op jit(solution)/shard_map/ppermute | solution.py:80
  188.5 10.0 %collective-permute-start.32 = (f32[112,256]{1,0:T(8,128)S(1)}, f32[112,256]{1,0:T(8,128)S(1)}, u32[]{:S(2)}, u32[]{:S(2)}) collective-permute-start(f32[112,256]{1,0:T(8,128)S(1)} %dynamic-slice_bitcast_fusion.8), channel_id=1, source_target_pairs={{0,8},{1,9},{2,10},{3,11},{4,12},{5,13},{6,14},{7,15},{8,0},{9,1},... | collective-permute-start | bytes 344072 | tf_op jit(solution)/shard_map/ppermute | solution.py:80
  198.5 6.7 %collective-permute-start.34 = (f32[112,256]{1,0:T(8,128)S(1)}, f32[112,256]{1,0:T(8,128)S(1)}, u32[]{:S(2)}, u32[]{:S(2)}) collective-permute-start(f32[112,256]{1,0:T(8,128)S(1)} %bitcast_add_fusion.5), channel_id=1, source_target_pairs={{0,8},{1,9},{2,10},{3,11},{4,12},{5,13},{6,14},{7,15},{8,0},{9,1},... | collective-permute-start | bytes 344072 | tf_op jit(solution)/shard_map/ppermute | solution.py:80
  205.3 7.6 %collective-permute-start.35 = (f32[224,256]{1,0:T(8,128)S(1)}, f32[224,256]{1,0:T(8,128)S(1)}, u32[]{:S(2)}, u32[]{:S(2)}) collective-permute-start(f32[224,256]{1,0:T(8,128)S(1)} %bitcast.307), channel_id=1, source_target_pairs={{0,4},{1,5},{2,6},{3,7},{4,0},{5,1},{6,2},{7,3},{8,12},{9,13},{10,... | collective-permute-start | bytes 688136 | tf_op jit(solution)/shard_map/ppermute | solution.py:80
  212.9 7.8 %collective-permute-start.36 = (f32[448,256]{1,0:T(8,128)S(1)}, f32[448,256]{1,0:T(8,128)S(1)}, u32[]{:S(2)}, u32[]{:S(2)}) collective-permute-start(f32[448,256]{1,0:T(8,128)S(1)} %bitcast.302), channel_id=1, source_target_pairs={{0,2},{1,3},{2,0},{3,1},{4,6},{5,7},{6,4},{7,5},{8,10},{9,11},{10,... | collective-permute-start | bytes 1376264 | tf_op jit(solution)/shard_map/ppermute | solution.py:80
  221.8 13.8 %collective-permute-start.37 = (f32[896,256]{1,0:T(8,128)}, f32[896,256]{1,0:T(8,128)}, u32[]{:S(2)}, u32[]{:S(2)}) collective-permute-start(f32[896,256]{1,0:T(8,128)} %bitcast.119), channel_id=1, source_target_pairs={{0,1},{1,0},{2,3},{3,2},{4,5},{5,4},{6,7},{7,6},{8,9},{9,8},{10,11... | collective-permute-start | bytes 2752520 | tf_op jit(solution)/shard_map/ppermute | solution.py:80
  229.6 6.0 %copy-start.11 = (bf16[4,1024]{1,0:T(4,128)(2,1)S(1)}, bf16[4,1024]{1,0:T(4,128)(2,1)}, u32[]{:S(2)}) copy-start(bf16[4,1024]{1,0:T(4,128)(2,1)} %param.23) | copy-start | bytes 24580
  229.6 53.3 %all-to-all-start = ((bf16[16,4,16,1024]{3,2,1,0:T(8,128)(2,1)}), bf16[16,4,16,1024]{3,2,1,0:T(8,128)(2,1)S(1)}, u32[]{:S(2)}, u32[]{:S(2)}) async-start(bf16[16,4,16,1024]{3,2,1,0:T(8,128)(2,1)} %bitcast.298), calls=%async_computation | async-start | bytes 4194304 | tf_op jit(solution)/shard_map/all_to_all | solution.py:503
  237.4 51.1 %copy-start.1 = (bf16[2048,64]{0,1:T(8,128)(2,1)S(1)}, bf16[2048,64]{0,1:T(8,128)(2,1)}, u32[]{:S(2)}) copy-start(bf16[2048,64]{0,1:T(8,128)(2,1)} %param.20) | copy-start | bytes 786436
  (9 other events, 11.2 us)
where the time goes:
time: 293 us; the launch traced here: 289 us
  waiting for transfers between devices  99.8 us (34%)
  Pallas kernels  72.4 us (25%)
  starting transfers between devices  50.5 us (17%)
  other arithmetic  28.4 us (10%)
  matrix products  22.5 us (8%)
  local copies, waits for them, and re-layouts  14.1 us (5%)
    ppermute x38, waiting for transfers between devices, exchange(): lax.ppermute(part, axis, [(i, i ^ bit) for i in range(lax.axis_size(axis))])  84.2 us
    pallas_call x5, Pallas kernels, kernel_call(): pl.pallas_call(kernel, out_shape=out, in_specs=[whole] * len(operands), o...  54.4 us
    ppermute x38, starting transfers between devices, exchange(): lax.ppermute(part, axis, [(i, i ^ bit) for i in range(lax.axis_size(axis))])  44.4 us
    all_to_all x1, waiting for transfers between devices, body(): lax.all_to_all(outgoing.reshape(device_count, lists_owned, slot_count, mo...  15.6 us
    another operation x43, other arithmetic, ordered(): return jnp.stack([jnp.where(low, part, other), jnp.where(low, other, part)])  12.4 us
    dot_general x1, matrix products, body(): nt(after(first_norm, *shrink_part), expand_rows)  12.4 us
    pallas_call x1, Pallas kernels, attend(): pl.pallas_call(functools.partial(attend_kernel, head_dim), grid=(steps,),...  9.11 us
    unnamed x37, local copies, waits for them, and re-layouts  6.63 us
  transfers between devices with their start and end apart: 39, of which 21 were waited for; matrix products, arithmetic and copies ran while one was open for 16% of the time, Pallas kernels for 23%

commit v1 on v0

--- a/solution.py
+++ b/solution.py
@@ -76,6 +76,49 @@
     )(segment[:, None], segment[None, :], projected, projected, projected)
 
 
+ERF_SHIFT = 0.3275911
+ERF_TERMS = (1.061405429, -1.453152027, 1.421413741, -0.284496736, 0.254829592)
+
+
+def gelu(value):
+    reach = jnp.abs(value) * math.sqrt(0.5)
+    below = 1.0 + ERF_SHIFT * reach
+    t = pl.reciprocal(below, approx=True)
+    t = t * (2.0 - below * t)
+    poly = ERF_TERMS[0]
+    for term in ERF_TERMS[1:]:
+        poly = poly * t + term
+    tail = 0.5 * value * (poly * t * jnp.exp2(reach * reach * -math.log2(math.e)))
+    return jnp.where(value < 0.0, tail, value - tail)
+
+
+def expand_kernel(rows_ref, weight_ref, out_ref):
+    product = lax.dot_general(
+        rows_ref[...], weight_ref[...], (((1,), (1,)), ((), ())), preferred_element_type=jnp.float32
+    )
+    out_ref[...] = gelu(product).astype(out_ref.dtype)
+
+
+def expand(rows, weight):
+    count, width = rows.shape
+    hidden = weight.shape[0]
+    tile = 256
+    return pl.pallas_call(
+        expand_kernel,
+        grid=(hidden // tile,),
+        in_specs=[
+            pl.BlockSpec((count, width), lambda i: (0, 0)),
+            pl.BlockSpec((tile, width), lambda i: (i, 0)),
+        ],
+        out_specs=pl.BlockSpec((count, tile), lambda i: (0, i)),
+        out_shape=jax.ShapeDtypeStruct((count, hidden), jnp.bfloat16),
+        compiler_params=pltpu.CompilerParams(vmem_limit_bytes=24 * 1024 * 1024),
+        cost_estimate=pl.CostEstimate(
+            flops=8 * count * width * hidden, bytes_accessed=8 << 20, transcendentals=2 * count * hidden
+        ),
+    )(rows, weight)
+
+
 def exchange(part, axis, bit):
     return lax.ppermute(part, axis, [(i, i ^ bit) for i in range(lax.axis_size(axis))])
 
@@ -105,10 +148,10 @@
     return lax.dynamic_index_in_dim(shares, lax.axis_index("groups"), 0, False)
 
 
-def gather_far(part, bits):
+def gather_far(part, bits, *beside):
     tail = part.shape[-3:]
     for bit in bits:
-        part = ordered(part, "dp", bit)
+        part = ordered(part, "dp", bit, *beside)
     return part.reshape((-1,) + tail)
 
 
@@ -374,28 +417,37 @@
     return ordered(part, "dp", bit, *beside).reshape(-1, part.shape[-1])
 
 
-def sum_first(part):
+def sum_both(first, second):
     bits = bits_of(lax.axis_size("dp"), 1)[::-1]
-    stages = [part]
-    for bit in bits[:-2]:
-        stages.append(halve(stages[-1], bit))
-    for bit in bits[-2:]:
-        stages.append(stages[-1] + exchange(stages[-1], "dp", bit))
-    for bit in bits[:-2][::-1]:
-        stages.append(rejoin(stages[-1], bit))
-    return stages[1:]
-
-
-def sum_second(part, sums, factors):
-    bits = bits_of(lax.axis_size("dp"), 1)[::-1]
-    gaps = [sums[k + (k >= len(bits) - 2)] for k in range(len(bits))] + [factors[0]]
-    for k, bit in enumerate(bits):
-        part = halve(part, bit, (gaps[k],), (gaps[k + 1],))
-    for k, bit in enumerate(bits[::-1]):
-        if bit == 2:
-            near = part
-        part = rejoin(part, bit, factors[min(k + 1, len(factors) - 1)])
-    return part, near
+    near, far = bits[:-2], bits[-2:]
+    first = halve(first, near[0])
+    second_sent = after(second, first)
+    for bit in near[1:]:
+        first = halve(first, bit)
+    second = halve(second_sent, bits[0], (), (first,))
+    first = first + after(exchange(first, "dp", far[0]), second)
+    second_next = functools.partial(halve, second, bits[1])
+    first = first + exchange(first, "dp", far[1])
+    second = second_next((), (first,))
+    first = rejoin(first, near[-1], second)
+    for bit in near[:-1][::-1]:
+        first = rejoin(first, bit)
+
+    def rest(besides, outgoing):
+        part, at = second, 0
+        for bit in bits[2:]:
+            part = halve(part, bit, (), besides[at : at + 1])
+            at += 1
+        for bit in bits[::-1]:
+            if bit == 2:
+                outgoing = after(outgoing, part)
+                part = rejoin(part, bit, outgoing)
+            else:
+                part = rejoin(part, bit, *besides[at : at + 1])
+            at += 1
+        return part, outgoing
+
+    return first, rest
 
 
 def filing_kernel(rows_ref, inverse_ref, centroids_ref, out_ref):
@@ -463,15 +515,16 @@
     near, far = far_bits[1:], far_bits[:1]
     input_part = gather_far(gather_far(own_share(input_weight.T), far), near)
     middle_part = gather_far(after(own_share(middle), input_part), far)
-    input_part = near_first(input_part)
-    middle_part = gather_far(after(middle_part, *input_part), near)
-    input_part = near_rest(*input_part)
-    shrink_part = gather_far(after(own_share(shrink_weight.T), *input_part), far)
-    middle_part = near_first(after(middle_part, *input_part))
+    input_first = near_first(input_part)
+    middle_part = gather_far(middle_part, near, *input_first)
+    shrink_part = gather_far(after(own_share(shrink_weight.T), middle_part), far)
+    input_part = near_rest(*input_first)
+    middle_first = near_first(middle_part, *input_part)
+    shrink_part = gather_far(shrink_part, near, *input_part)
     projected = nt(gather_cores(*input_part), tokens).astype(jnp.bfloat16)
-    shrink_part = gather_far(after(shrink_part, *middle_part), near)
-    attended = attend(after(projected, *middle_part), segment_ids(lengths[0], row_count))
-    middle_part = near_rest(*middle_part, attended)
+    attended = attend(after(projected, *middle_first), segment_ids(lengths[0], row_count))
+    middle_part = near_rest(*middle_first, attended)
+    shrink_first = near_first(after(shrink_part, *middle_first), attended)
     middle_rows = gather_cores(*middle_part).reshape(device_count, -1, model_width)
     own_output = output_weight.shape[1]
     output_rows = middle_rows[:, :own_output].reshape(-1, model_width)
@@ -480,9 +533,8 @@
         attended, output_rows, (((0,), (1,)), ((), ())), preferred_element_type=jnp.float32
     )
     first_norm = layer_norm(tokens.astype(jnp.float32) + mixed_out, norm_gain).astype(jnp.bfloat16)
-    shrink_part = near_first(after(shrink_part, *middle_part), first_norm)
-    expanded = jax.nn.gelu(nt(after(first_norm, *shrink_part), expand_rows), approximate=False).astype(jnp.bfloat16)
-    shrink_part = near_rest(*shrink_part, expanded)
+    expanded = expand(after(first_norm, *shrink_first), expand_rows)
+    shrink_part = near_rest(*shrink_first, expanded)
     shrink_rows = gather_cores(*shrink_part)
     reduced = nt(expanded, shrink_rows)
     embedded = layer_norm(first_norm.astype(jnp.float32) + reduced, 1.0).astype(jnp.bfloat16)
@@ -494,12 +546,12 @@
     scale = 1.0 / (row_count * device_count)
     first_tiles = gram_tiles(embedded, FIRST_TILES)
     second_tiles = gram_tiles(after(embedded, first_tiles), SECOND_TILES)
-    sums = sum_first(first_tiles.reshape(-1, first_tiles.shape[-1]))
-    stages = inverse_first(sums[-1].reshape(first_tiles.shape), scale, ridge_term)
-    second_sum, near = sum_second(second_tiles.reshape(-1, second_tiles.shape[-1]), sums, stages)
+    flat = functools.partial(jnp.reshape, shape=(-1, first_tiles.shape[-1]))
+    first_sum, rest = sum_both(flat(first_tiles), flat(second_tiles))
+    stages = inverse_first(first_sum.reshape(first_tiles.shape), scale, ridge_term)
+    second_sum, outgoing = rest(stages, outgoing)
     second_sum = second_sum.reshape(second_tiles.shape)
     first = stages[-1]
-    outgoing = after(outgoing, near)
     incoming = lax.all_to_all(
         outgoing.reshape(device_count, lists_owned, slot_count, model_width),
         "dp",

time: 293 us -> 274 us (0.935)
  waiting for transfers between devices: 99.8 us -> 88.1 us
  matrix products: 22.5 us -> 11.5 us
  Pallas kernels: 72.4 us -> 78.7 us
  other arithmetic: 28.4 us -> 22.2 us
  starting transfers between devices: 50.5 us -> 53.9 us
    dot_general x1 -> x0, matrix products: 12.4 us -> none  [body(): nt(after(first_norm, *shrink_part), expand_rows)]
    ppermute x38, waiting for transfers between devices: 84.2 us -> 72.7 us  [exchange(): lax.ppermute(part, axis, [(i, i ^ bit) for i in range(lax.axis_size(axis))])]
    pallas_call x0 -> x1, Pallas kernels: none -> 6.74 us  [expand(): pl.pallas_call(expand_kernel, grid=(hidden // tile,), in_specs=[pl.BlockS...]
    ppermute x38, starting transfers between devices: 44.4 us -> 48.1 us  [exchange(): lax.ppermute(part, axis, [(i, i ^ bit) for i in range(lax.axis_size(axis))])]
    another operation x43, other arithmetic: 12.4 us -> 8.84 us  [ordered(): return jnp.stack([jnp.where(low, part, other), jnp.where(low, other, part)])]
    unnamed x37 -> x51, local copies, waits for them, and re-layouts: 6.63 us -> 7.72 us
  transfers between devices with their start and end apart: 39 -> 39, of which waited for: 21 -> 18; matrix products, arithmetic and copies ran while one was open for 16% -> 11% of each run, Pallas kernels for 23% -> 27%
where the time goes in v1:
time: 274 us; the launch traced here: 270 us
  waiting for transfers between devices  88.1 us (32%)
  Pallas kernels  78.7 us (29%)
  starting transfers between devices  53.9 us (20%)
  other arithmetic  22.2 us (8%)
  local copies, waits for them, and re-layouts  14.9 us (5%)
  matrix products  11.5 us (4%)
    ppermute x38, waiting for transfers between devices, exchange(): lax.ppermute(part, axis, [(i, i ^ bit) for i in range(lax.axis_size(axis))])  72.7 us
    pallas_call x5, Pallas kernels, kernel_call(): pl.pallas_call(kernel, out_shape=out, in_specs=[whole] * len(operands), o...  54.2 us
    ppermute x38, starting transfers between devices, exchange(): lax.ppermute(part, axis, [(i, i ^ bit) for i in range(lax.axis_size(axis))])  48.1 us
    all_to_all x1, waiting for transfers between devices, body(): lax.all_to_all(outgoing.reshape(device_count, lists_owned, slot_count, mo...  15.4 us
    pallas_call x1, Pallas kernels, attend(): pl.pallas_call(functools.partial(attend_kernel, head_dim), grid=(steps,),...  9.11 us
    another operation x43, other arithmetic, ordered(): return jnp.stack([jnp.where(low, part, other), jnp.where(low, other, part)])  8.84 us
    unnamed x51, local copies, waits for them, and re-layouts  7.72 us
    pallas_call x1, Pallas kernels, expand(): pl.pallas_call(expand_kernel, grid=(hidden // tile,), in_specs=[pl.BlockS...  6.74 us
  transfers between devices with their start and end apart: 39, of which 18 were waited for; matrix products, arithmetic and copies ran while one was open for 11% of the time, Pallas kernels for 27%

profile of v1, /device:TPU:13, one launch (start us, length us, event | category | flops | bytes accessed | tf_op | source)
XLA Modules:
  0.0 270.2 jit_solution(2161822545665912080)
XLA Ops:
  1.0 2.4 collective-permute-start
  4.5 7.6 %collective-permute-done = bf16[2,48,1024]{2,1,0:T(8,128)(2,1)S(1)} collective-permute-done((bf16[2,48,1024]{2,1,0:T(8,128)(2,1)S(1)}, bf16[2,48,1024]{2,1,0:T(8,128)(2,1)S(1)}, u32[]{:S(2)}, u32[]{:S(2)}) %collective-permute-start) | collective-permute-done | bytes 196640 | tf_op jit(solution)/shard_map/ppermute | solution.py:123
  13.5 9.8 %collective-permute-done.1 = bf16[2,2,48,1024]{3,2,1,0:T(8,128)(2,1)S(1)} collective-permute-done((bf16[2,2,48,1024]{3,2,1,0:T(8,128)(2,1)S(1)}, bf16[2,2,48,1024]{3,2,1,0:T(8,128)(2,1)S(1)}, u32[]{:S(2)}, u32[]{:S(2)}) %collective-permute-start.1) | collective-permute-done | bytes 393248 | tf_op jit(solution)/shard_map/ppermute | solution.py:123
  23.5 3.2 %collective-permute-start.8 = (bf16[2,48,1024]{2,1,0:T(8,128)(2,1)S(1)}, bf16[2,48,1024]{2,1,0:T(8,128)(2,1)S(1)}, u32[]{:S(2)}, u32[]{:S(2)}) collective-permute-start(bf16[2,48,1024]{2,1,0:T(8,128)(2,1)S(1)} %dynamic-slice_bitcast_fusion.5), channel_id=1, source_target_pairs={{0,8},{1,9},{2,10},{3,11},{4,12},{5,13},{6,14},{7,15},{8,0},{9,1},... | collective-permute-start | bytes 589832 | tf_op jit(solution)/shard_map/ppermute | solution.py:123
  28.5 7.0 %collective-permute-done.8 = bf16[2,48,1024]{2,1,0:T(8,128)(2,1)S(1)} collective-permute-done((bf16[2,48,1024]{2,1,0:T(8,128)(2,1)S(1)}, bf16[2,48,1024]{2,1,0:T(8,128)(2,1)S(1)}, u32[]{:S(2)}, u32[]{:S(2)}) %collective-permute-start.8) | collective-permute-done | bytes 196640 | tf_op jit(solution)/shard_map/ppermute | solution.py:123
  38.6 7.2 %collective-permute-done.9 = bf16[2,2,48,1024]{3,2,1,0:T(8,128)(2,1)S(1)} collective-permute-done((bf16[2,2,48,1024]{3,2,1,0:T(8,128)(2,1)S(1)}, bf16[2,2,48,1024]{3,2,1,0:T(8,128)(2,1)S(1)}, u32[]{:S(2)}, u32[]{:S(2)}) %collective-permute-start.9) | collective-permute-done | bytes 393248 | tf_op jit(solution)/shard_map/ppermute | solution.py:123
  45.9 3.2 %collective-permute-start.16 = (bf16[2,16,2048]{2,1,0:T(8,128)(2,1)S(1)}, bf16[2,16,2048]{2,1,0:T(8,128)(2,1)S(1)}, u32[]{:S(2)}, u32[]{:S(2)}) collective-permute-start(bf16[2,16,2048]{2,1,0:T(8,128)(2,1)S(1)} %dynamic-slice_bitcast_fusion.7), channel_id=1, source_target_pairs={{0,8},{1,9},{2,10},{3,11},{4,12},{5,13},{6,14},{7,15},{8,0},{9,1},... | collective-permute-start | bytes 393224 | tf_op jit(solution)/shard_map/ppermute | solution.py:123
  50.6 4.4 %collective-permute-done.16 = bf16[2,16,2048]{2,1,0:T(8,128)(2,1)S(1)} collective-permute-done((bf16[2,16,2048]{2,1,0:T(8,128)(2,1)S(1)}, bf16[2,16,2048]{2,1,0:T(8,128)(2,1)S(1)}, u32[]{:S(2)}, u32[]{:S(2)}) %collective-permute-start.16) | collective-permute-done | bytes 131104 | tf_op jit(solution)/shard_map/ppermute | solution.py:123
  55.7 4.0 %collective-permute-start.4 = (bf16[2,2,4,48,1024]{4,3,2,1,0:T(8,128)(2,1)S(1)}, bf16[2,2,4,48,1024]{4,3,2,1,0:T(8,128)(2,1)S(1)}, u32[]{:S(2)}, u32[]{:S(2)}) collective-permute-start(bf16[2,2,4,48,1024]{4,3,2,1,0:T(8,128)(2,1)S(1)} %pad_maximum_fusion.1), channel_id=1, source_target_pairs={{0,1},{1,0},{2,3},{3,2},{4,5},{5,4},{6,7},{7,6},{8,9},{9,8},{10,11... | collective-permute-start | bytes 4718600 | tf_op jit(solution)/shard_map/ppermute | solution.py:123
  59.9 1.4 collective-permute-start.7
  67.7 1.3 copy.82
  69.0 5.0 %convolution_convert_fusion.query_ref.key_ref.value_ref = bf16[3072,512]{1,0:T(8,128)(2,1)S(1)} fusion(bf16[3072,1024]{1,0:T(8,128)(2,1)S(1)} %bitcast.283, bf16[512,1024]{1,0:T(8,128)(2,1)} %param.14), kind=kOutput, calls=%fused_computation.2 | convolution fusion | flops 3222798336 | bytes 10485760 | tf_op jit(solution)/shard_map/dot_general | solution.py:524
  74.0 9.1 %shard_map.136 = bf16[1024,512]{1,0:T(8,128)(2,1)S(1)} custom-call(s32[512,1]{1,0:T(8,128)S(1)} %copy.85.column_ref, s32[1,512]{1,0:T(1,128)S(1)} %bitcast.272, bf16[3072,512]{1,0:T(8,128)(2,1)S(1)} %convolution_convert_fusion.query_ref.key_ref.value_ref, bf16[3072,512]{1,0:T(8,128)(2,1)S(1)} %convolution_convert_fusion.query_ref.key_ref.value_ref, ...), custom_call_target="tpu_custom_call" | custom-call | flops 1073741824 | bytes 4194304 | tf_op jit(solution)/shard_map/pallas_call | solution.py:57
  84.0 2.0 collective-permute-done.18
  86.3 3.7 %collective-permute-start.13 = (bf16[2,2,4,48,1024]{4,3,2,0,1:T(8,128)(2,1)S(1)}, bf16[2,2,4,48,1024]{4,3,2,0,1:T(8,128)(2,1)S(1)}, u32[]{:S(2)}, u32[]{:S(2)}) collective-permute-start(bf16[2,2,4,48,1024]{4,3,2,0,1:T(8,128)(2,1)S(1)} %pad_maximum_fusion.2), channel_id=1, source_target_pairs={{0,1},{1,0},{2,3},{3,2},{4,5},{5,4},{6,7},{7,6},{8,9},{9,8},{10,11... | collective-permute-start | bytes 4718600 | tf_op jit(solution)/shard_map/ppermute | solution.py:123
  93.6 1.7 collective-permute-done.15
  99.2 1.4 fusion.3
  101.6 6.7 %shard_map.137 = bf16[512,2048]{1,0:T(8,128)(2,1)S(1)} custom-call(bf16[512,1024]{1,0:T(8,128)(2,1)S(1)} %multiply_convert_fusion.1.rows_ref, bf16[2048,1024]{1,0:T(8,128)(2,1)S(1)} %bitcast.266), custom_call_target="tpu_custom_call" | custom-call | flops 8589934592 | bytes 8388608 | tf_op jit(solution)/shard_map/pallas_call | solution.py:106
  113.3 1.7 broadcast_select_fusion.11
  115.7 1.4 broadcast_select_fusion.9
  118.2 2.5 fusion.4
  121.7 1.6 shard_map.138
  124.5 3.0 %shard_map.139 = f32[7,256,256]{2,1,0:T(8,128)S(1)} custom-call(s32[7]{0:T(128)S(1)} %copy-done.6, s32[7]{0:T(128)S(1)} %copy-done.7, bf16[512,1024]{1,0:T(8,128)(2,1)S(1)} %multiply_convert_fusion.left_ref.right_ref, bf16[512,1024]{1,0:T(8,128)(2,1)S(1)} %multiply_convert_fusion.left_ref.right_ref), custom_call_target="tpu_custom_call" | custom-call | flops 469762048 | bytes 4194304 | tf_op jit(solution)/shard_map/pallas_call | solution.py:389
  130.3 6.2 %collective-permute-done.26 = f32[192,256]{1,0:T(8,128)} collective-permute-done((f32[192,256]{1,0:T(8,128)S(1)}, f32[192,256]{1,0:T(8,128)}, u32[]{:S(2)}, u32[]{:S(2)}) %collective-permute-start.26) | collective-permute-done | bytes 196640 | tf_op jit(solution)/shard_map/ppermute | solution.py:123
  137.5 1.3 bitcast_add_fusion
  139.1 1.3 collective-permute-start.28
  140.4 3.8 %collective-permute-done.28 = f32[192,256]{1,0:T(8,128)S(1)} collective-permute-done((f32[192,256]{1,0:T(8,128)S(1)}, f32[192,256]{1,0:T(8,128)S(1)}, u32[]{:S(2)}, u32[]{:S(2)}) %collective-permute-start.28) | collective-permute-done | bytes 196640 | tf_op jit(solution)/shard_map/ppermute | solution.py:123
  144.3 4.3 %collective-permute-start.29 = (f32[192,256]{1,0:T(8,128)S(1)}, f32[192,256]{1,0:T(8,128)S(1)}, u32[]{:S(2)}, u32[]{:S(2)}) collective-permute-start(f32[192,256]{1,0:T(8,128)S(1)} %add.168), channel_id=1, source_target_pairs={{0,8},{1,9},{2,10},{3,11},{4,12},{5,13},{6,14},{7,15},{8,0},{9,1},... | collective-permute-start | bytes 589832 | tf_op jit(solution)/shard_map/ppermute | solution.py:123
  148.6 7.9 %collective-permute-done.29 = f32[192,256]{1,0:T(8,128)S(1)} collective-permute-done((f32[192,256]{1,0:T(8,128)S(1)}, f32[192,256]{1,0:T(8,128)S(1)}, u32[]{:S(2)}, u32[]{:S(2)}) %collective-permute-start.29) | collective-permute-done | bytes 196640 | tf_op jit(solution)/shard_map/ppermute | solution.py:123
  157.4 4.3 %collective-permute-done.31 = f32[192,256]{1,0:T(8,128)S(1)} collective-permute-done((f32[192,256]{1,0:T(8,128)S(1)}, f32[192,256]{1,0:T(8,128)S(1)}, u32[]{:S(2)}, u32[]{:S(2)}) %collective-permute-start.31) | collective-permute-done | bytes 196640 | tf_op jit(solution)/shard_map/ppermute | solution.py:123
  161.8 2.4 collective-permute-start.32
  164.5 2.7 collective-permute-start.30
  167.3 6.7 %shard_map.140.work_ref = f32[512,512]{1,0:T(8,128)S(1)} custom-call(f32[3,256,256]{2,1,0:T(8,128)S(1)} %bitcast.270), custom_call_target="tpu_custom_call" | custom-call | flops 7500000256 | bytes 4194304 | tf_op jit(solution)/shard_map/pallas_call | solution.py:334
  174.1 1.5 collective-permute-start.33
  175.6 6.6 %shard_map.141.work_ref = f32[512,512]{1,0:T(8,128)S(1)} custom-call(f32[512,512]{1,0:T(8,128)S(1)} %shard_map.140.work_ref), custom_call_target="tpu_custom_call" | custom-call | flops 7500000256 | bytes 4194304 | tf_op jit(solution)/shard_map/pallas_call | solution.py:334
  182.2 1.6 collective-permute-start.34
  183.8 6.7 %shard_map.142.work_ref = f32[512,512]{1,0:T(8,128)S(1)} custom-call(f32[512,512]{1,0:T(8,128)S(1)} %shard_map.141.work_ref), custom_call_target="tpu_custom_call" | custom-call | flops 7500000256 | bytes 4194304 | tf_op jit(solution)/shard_map/pallas_call | solution.py:334
  191.7 5.7 %shard_map.143.first_ref = f32[512,512]{1,0:T(8,128)S(1)} custom-call(f32[512,512]{1,0:T(8,128)S(1)} %shard_map.142.work_ref), custom_call_target="tpu_custom_call" | custom-call | flops 7500000256 | bytes 4194304 | tf_op jit(solution)/shard_map/pallas_call | solution.py:334
  198.5 2.6 select_convert_fusion
  201.1 7.2 %collective-permute-done.36 = f32[448,256]{1,0:T(8,128)S(1)} collective-permute-done((f32[448,256]{1,0:T(8,128)S(1)}, f32[448,256]{1,0:T(8,128)S(1)}, u32[]{:S(2)}, u32[]{:S(2)}) %collective-permute-start.36) | collective-permute-done | bytes 458784 | tf_op jit(solution)/shard_map/ppermute | solution.py:123
  209.4 2.2 collective-permute-start.37
  211.6 5.8 %all-to-all-start = ((bf16[16,4,16,1024]{3,2,1,0:T(8,128)(2,1)}), bf16[16,4,16,1024]{3,2,1,0:T(8,128)(2,1)S(1)}, u32[]{:S(2)}, u32[]{:S(2)}) async-start(bf16[16,4,16,1024]{3,2,1,0:T(8,128)(2,1)} %bitcast.299), calls=%async_computation | async-start | bytes 4194304 | tf_op jit(solution)/shard_map/all_to_all | solution.py:555
  217.5 1.6 select_bitcast_fusion.1
  219.2 28.5 %shard_map.144.inverse_ref = bf16[1024,1024]{1,0:T(8,128)(2,1)S(1)} custom-call(f32[512,512]{1,0:T(8,128)S(1)} %shard_map.143.first_ref, f32[7,256,256]{2,1,0:T(8,128)S(1)} %bitcast.269), custom_call_target="tpu_custom_call" | custom-call | flops 30000001024 | bytes 4194304 | tf_op jit(solution)/shard_map/pallas_call | solution.py:334
  247.8 1.3 copy-done.4
  249.1 15.4 %all-to-all-done.rows_ref = bf16[16,4,16,1024]{3,2,1,0:T(8,128)(2,1)S(1)} async-done(((bf16[16,4,16,1024]{3,2,1,0:T(8,128)(2,1)}), bf16[16,4,16,1024]{3,2,1,0:T(8,128)(2,1)S(1)}, u32[]{:S(2)}, u32[]{:S(2)}) %all-to-all-start) | async-done | bytes 2097184 | tf_op jit(solution)/shard_map/all_to_all | solution.py:555
  264.5 1.6 copy-done.5
  266.1 4.0 %shard_map.145 = bf16[4,256,1024]{2,1,0:T(8,128)(2,1)} custom-call(bf16[16,4,16,1024]{3,2,1,0:T(8,128)(2,1)S(1)} %all-to-all-done.rows_ref, bf16[1024,1024]{1,0:T(8,128)(2,1)S(1)} %copy-done.5, bf16[4,1,1024]{2,1,0:T(2,128)(2,1)S(1)} %copy.98.centroids_ref), custom_call_target="tpu_custom_call" | custom-call | tf_op jit(solution)/shard_map/pallas_call | solution.py:463
  (196 shorter events, 44.6 us)
Async XLA Ops:
  0.0 13.5 %copy-start = (bf16[2048,64]{0,1:T(8,128)(2,1)S(1)}, bf16[2048,64]{0,1:T(8,128)(2,1)}, u32[]{:S(2)}) copy-start(bf16[2048,64]{0,1:T(8,128)(2,1)} %param.20) | copy-start | bytes 786436
  0.0 13.2 %copy-start.18 = (bf16[1024,64]{0,1:T(8,128)(2,1)S(1)}, bf16[1024,64]{0,1:T(8,128)(2,1)}, u32[]{:S(2)}) copy-start(bf16[1024,64]{0,1:T(8,128)(2,1)} %param.17) | copy-start | bytes 393220
  0.0 13.3 %copy-start.24 = (s32[1,8]{1,0:T(1,128)S(1)}, s32[1,8]{1,0:T(1,128)}, u32[]{:S(2)}) copy-start(s32[1,8]{1,0:T(1,128)} %param.15) | copy-start | bytes 100
  1.0 11.1 %collective-permute-start = (bf16[2,48,1024]{2,1,0:T(8,128)(2,1)S(1)}, bf16[2,48,1024]{2,1,0:T(8,128)(2,1)S(1)}, u32[]{:S(2)}, u32[]{:S(2)}) collective-permute-start(bf16[2,48,1024]{2,1,0:T(8,128)(2,1)S(1)} %dynamic-slice_bitcast_fusion.6), channel_id=1, source_target_pairs={{0,8},{1,9},{2,10},{3,11},{4,12},{5,13},{6,14},{7,15},{8,0},{9,1},... | collective-permute-start | bytes 589832 | tf_op jit(solution)/shard_map/ppermute | solution.py:123
  13.1 10.3 %collective-permute-start.1 = (bf16[2,2,48,1024]{3,2,1,0:T(8,128)(2,1)S(1)}, bf16[2,2,48,1024]{3,2,1,0:T(8,128)(2,1)S(1)}, u32[]{:S(2)}, u32[]{:S(2)}) collective-permute-start(bf16[2,2,48,1024]{3,2,1,0:T(8,128)(2,1)S(1)} %pad_maximum_fusion.16), channel_id=1, source_target_pairs={{0,4},{1,5},{2,6},{3,7},{4,0},{5,1},{6,2},{7,3},{8,12},{9,13},{10,... | collective-permute-start | bytes 1179656 | tf_op jit(solution)/shard_map/ppermute | solution.py:123
  23.5 12.0 %collective-permute-start.8 = (bf16[2,48,1024]{2,1,0:T(8,128)(2,1)S(1)}, bf16[2,48,1024]{2,1,0:T(8,128)(2,1)S(1)}, u32[]{:S(2)}, u32[]{:S(2)}) collective-permute-start(bf16[2,48,1024]{2,1,0:T(8,128)(2,1)S(1)} %dynamic-slice_bitcast_fusion.5), channel_id=1, source_target_pairs={{0,8},{1,9},{2,10},{3,11},{4,12},{5,13},{6,14},{7,15},{8,0},{9,1},... | collective-permute-start | bytes 589832 | tf_op jit(solution)/shard_map/ppermute | solution.py:123
  26.7 9.1 %collective-permute-start.2 = (bf16[4,48,1024]{2,1,0:T(8,128)(2,1)S(1)}, bf16[4,48,1024]{2,1,0:T(8,128)(2,1)S(1)}, u32[]{:S(2)}, u32[]{:S(2)}) collective-permute-start(bf16[4,48,1024]{2,1,0:T(8,128)(2,1)S(1)} %get-tuple-element.109), channel_id=1, source_target_pairs={{0,2},{1,3},{2,0},{3,1},{4,6},{5,7},{6,4},{7,5},{8,10},{9,11},{10,... | collective-permute-start | bytes 1179656 | tf_op jit(solution)/shard_map/ppermute | solution.py:123
  27.0 8.8 %collective-permute-start.5 = (bf16[4,48,1024]{2,1,0:T(8,128)(2,1)S(1)}, bf16[4,48,1024]{2,1,0:T(8,128)(2,1)S(1)}, u32[]{:S(2)}, u32[]{:S(2)}) collective-permute-start(bf16[4,48,1024]{2,1,0:T(8,128)(2,1)S(1)} %get-tuple-element.110), channel_id=1, source_target_pairs={{0,16},{16,0},{1,17},{17,1},{2,18},{18,2},{3,19},{19,3},{4,20},{20... | collective-permute-start | bytes 1179656 | tf_op jit(solution)/shard_map/ppermute | solution.py:123
  35.6 10.2 %collective-permute-start.9 = (bf16[2,2,48,1024]{3,2,1,0:T(8,128)(2,1)S(1)}, bf16[2,2,48,1024]{3,2,1,0:T(8,128)(2,1)S(1)}, u32[]{:S(2)}, u32[]{:S(2)}) collective-permute-start(bf16[2,2,48,1024]{3,2,1,0:T(8,128)(2,1)S(1)} %pad_maximum_fusion.18), channel_id=1, source_target_pairs={{0,4},{1,5},{2,6},{3,7},{4,0},{5,1},{6,2},{7,3},{8,12},{9,13},{10,... | collective-permute-start | bytes 1179656 | tf_op jit(solution)/shard_map/ppermute | solution.py:123
  36.0 19.4 %collective-permute-start.3 = (bf16[2,4,48,1024]{3,2,1,0:T(8,128)(2,1)S(1)}, bf16[2,4,48,1024]{3,2,1,0:T(8,128)(2,1)S(1)}, u32[]{:S(2)}, u32[]{:S(2)}) collective-permute-start(bf16[2,4,48,1024]{3,2,1,0:T(8,128)(2,1)S(1)} %pad_maximum_fusion.6), channel_id=1, source_target_pairs={{0,16},{16,0},{1,17},{17,1},{2,18},{18,2},{3,19},{19,3},{4,20},{20... | collective-permute-start | bytes 2359304 | tf_op jit(solution)/shard_map/ppermute | solution.py:123
  37.4 22.2 %collective-permute-start.6 = (bf16[2,4,48,1024]{3,2,1,0:T(8,128)(2,1)S(1)}, bf16[2,4,48,1024]{3,2,1,0:T(8,128)(2,1)S(1)}, u32[]{:S(2)}, u32[]{:S(2)}) collective-permute-start(bf16[2,4,48,1024]{3,2,1,0:T(8,128)(2,1)S(1)} %pad_maximum_fusion.7), channel_id=1, source_target_pairs={{0,2},{1,3},{2,0},{3,1},{4,6},{5,7},{6,4},{7,5},{8,10},{9,11},{10,... | collective-permute-start | bytes 2359304 | tf_op jit(solution)/shard_map/ppermute | solution.py:123
  45.9 9.1 %collective-permute-start.16 = (bf16[2,16,2048]{2,1,0:T(8,128)(2,1)S(1)}, bf16[2,16,2048]{2,1,0:T(8,128)(2,1)S(1)}, u32[]{:S(2)}, u32[]{:S(2)}) collective-permute-start(bf16[2,16,2048]{2,1,0:T(8,128)(2,1)S(1)} %dynamic-slice_bitcast_fusion.7), channel_id=1, source_target_pairs={{0,8},{1,9},{2,10},{3,11},{4,12},{5,13},{6,14},{7,15},{8,0},{9,1},... | collective-permute-start | bytes 393224 | tf_op jit(solution)/shard_map/ppermute | solution.py:123
  49.1 13.3 %collective-permute-start.10 = (bf16[4,48,1024]{2,1,0:T(8,128)(2,1)S(1)}, bf16[4,48,1024]{2,1,0:T(8,128)(2,1)S(1)}, u32[]{:S(2)}, u32[]{:S(2)}) collective-permute-start(bf16[4,48,1024]{2,1,0:T(8,128)(2,1)S(1)} %get-tuple-element.104), channel_id=1, source_target_pairs={{0,2},{1,3},{2,0},{3,1},{4,6},{5,7},{6,4},{7,5},{8,10},{9,11},{10,... | collective-permute-start | bytes 1179656 | tf_op jit(solution)/shard_map/ppermute | solution.py:123
  49.4 13.0 %collective-permute-start.11 = (bf16[4,48,1024]{2,1,0:T(8,128)(2,1)S(1)}, bf16[4,48,1024]{2,1,0:T(8,128)(2,1)S(1)}, u32[]{:S(2)}, u32[]{:S(2)}) collective-permute-start(bf16[4,48,1024]{2,1,0:T(8,128)(2,1)S(1)} %get-tuple-element.103), channel_id=1, source_target_pairs={{0,16},{16,0},{1,17},{17,1},{2,18},{18,2},{3,19},{19,3},{4,20},{20... | collective-permute-start | bytes 1179656 | tf_op jit(solution)/shard_map/ppermute | solution.py:123
  55.1 7.4 %collective-permute-start.17 = (bf16[2,2,16,2048]{3,2,1,0:T(8,128)(2,1)S(1)}, bf16[2,2,16,2048]{3,2,1,0:T(8,128)(2,1)S(1)}, u32[]{:S(2)}, u32[]{:S(2)}) collective-permute-start(bf16[2,2,16,2048]{3,2,1,0:T(8,128)(2,1)S(1)} %pad_maximum_fusion.20), channel_id=1, source_target_pairs={{0,4},{1,5},{2,6},{3,7},{4,0},{5,1},{6,2},{7,3},{8,12},{9,13},{10,... | collective-permute-start | bytes 786440 | tf_op jit(solution)/shard_map/ppermute | solution.py:123
  55.7 9.4 %collective-permute-start.4 = (bf16[2,2,4,48,1024]{4,3,2,1,0:T(8,128)(2,1)S(1)}, bf16[2,2,4,48,1024]{4,3,2,1,0:T(8,128)(2,1)S(1)}, u32[]{:S(2)}, u32[]{:S(2)}) collective-permute-start(bf16[2,2,4,48,1024]{4,3,2,1,0:T(8,128)(2,1)S(1)} %pad_maximum_fusion.1), channel_id=1, source_target_pairs={{0,1},{1,0},{2,3},{3,2},{4,5},{5,4},{6,7},{7,6},{8,9},{9,8},{10,11... | collective-permute-start | bytes 4718600 | tf_op jit(solution)/shard_map/ppermute | solution.py:123
  59.9 6.2 %collective-permute-start.7 = (bf16[2,2,4,48,1024]{4,3,2,1,0:T(8,128)(2,1)S(1)}, bf16[2,2,4,48,1024]{4,3,2,1,0:T(8,128)(2,1)S(1)}, u32[]{:S(2)}, u32[]{:S(2)}) collective-permute-start(bf16[2,2,4,48,1024]{4,3,2,1,0:T(8,128)(2,1)S(1)} %maximum_bitcast_fusion.2), channel_id=1, source_target_pairs={{0,1},{1,0},{2,3},{3,2},{4,5},{5,4},{6,7},{7,6},{8,9},{9,8},{10,11... | collective-permute-start | bytes 4718600 | tf_op jit(solution)/shard_map/ppermute | solution.py:123
  62.6 23.4 %collective-permute-start.12 = (bf16[2,4,48,1024]{3,2,1,0:T(8,128)(2,1)S(1)}, bf16[2,4,48,1024]{3,2,1,0:T(8,128)(2,1)S(1)}, u32[]{:S(2)}, u32[]{:S(2)}) collective-permute-start(bf16[2,4,48,1024]{3,2,1,0:T(8,128)(2,1)S(1)} %pad_maximum_fusion.9), channel_id=1, source_target_pairs={{0,16},{16,0},{1,17},{17,1},{2,18},{18,2},{3,19},{19,3},{4,20},{20... | collective-permute-start | bytes 2359304 | tf_op jit(solution)/shard_map/ppermute | solution.py:123
  64.0 26.0 %collective-permute-start.14 = (bf16[2,4,48,1024]{3,2,1,0:T(8,128)(2,1)S(1)}, bf16[2,4,48,1024]{3,2,1,0:T(8,128)(2,1)S(1)}, u32[]{:S(2)}, u32[]{:S(2)}) collective-permute-start(bf16[2,4,48,1024]{3,2,1,0:T(8,128)(2,1)S(1)} %pad_maximum_fusion.10), channel_id=1, source_target_pairs={{0,2},{1,3},{2,0},{3,1},{4,6},{5,7},{6,4},{7,5},{8,10},{9,11},{10,... | collective-permute-start | bytes 2359304 | tf_op jit(solution)/shard_map/ppermute | solution.py:123
  64.4 19.5 %collective-permute-start.19 = (bf16[4,16,2048]{2,1,0:T(8,128)(2,1)S(1)}, bf16[4,16,2048]{2,1,0:T(8,128)(2,1)S(1)}, u32[]{:S(2)}, u32[]{:S(2)}) collective-permute-start(bf16[4,16,2048]{2,1,0:T(8,128)(2,1)S(1)} %slice_bitcast_fusion.5), channel_id=1, source_target_pairs={{0,16},{16,0},{1,17},{17,1},{2,18},{18,2},{3,19},{19,3},{4,20},{20... | collective-permute-start | bytes 786440 | tf_op jit(solution)/shard_map/ppermute | solution.py:123
  65.1 20.9 %collective-permute-start.18 = (bf16[4,16,2048]{2,1,0:T(8,128)(2,1)S(1)}, bf16[4,16,2048]{2,1,0:T(8,128)(2,1)S(1)}, u32[]{:S(2)}, u32[]{:S(2)}) collective-permute-start(bf16[4,16,2048]{2,1,0:T(8,128)(2,1)S(1)} %slice_bitcast_fusion.4), channel_id=1, source_target_pairs={{0,2},{1,3},{2,0},{3,1},{4,6},{5,7},{6,4},{7,5},{8,10},{9,11},{10,... | collective-permute-start | bytes 786440 | tf_op jit(solution)/shard_map/ppermute | solution.py:123
  86.3 6.7 %collective-permute-start.13 = (bf16[2,2,4,48,1024]{4,3,2,0,1:T(8,128)(2,1)S(1)}, bf16[2,2,4,48,1024]{4,3,2,0,1:T(8,128)(2,1)S(1)}, u32[]{:S(2)}, u32[]{:S(2)}) collective-permute-start(bf16[2,2,4,48,1024]{4,3,2,0,1:T(8,128)(2,1)S(1)} %pad_maximum_fusion.2), channel_id=1, source_target_pairs={{0,1},{1,0},{2,3},{3,2},{4,5},{5,4},{6,7},{7,6},{8,9},{9,8},{10,11... | collective-permute-start | bytes 4718600 | tf_op jit(solution)/shard_map/ppermute | solution.py:123
  90.3 5.0 %collective-permute-start.15 = (bf16[2,2,4,48,1024]{4,3,2,0,1:T(8,128)(2,1)S(1)}, bf16[2,2,4,48,1024]{4,3,2,0,1:T(8,128)(2,1)S(1)}, u32[]{:S(2)}, u32[]{:S(2)}) collective-permute-start(bf16[2,2,4,48,1024]{4,3,2,0,1:T(8,128)(2,1)S(1)} %maximum_bitcast_fusion.3), channel_id=1, source_target_pairs={{0,1},{1,0},{2,3},{3,2},{4,5},{5,4},{6,7},{7,6},{8,9},{9,8},{10,11... | collective-permute-start | bytes 4718600 | tf_op jit(solution)/shard_map/ppermute | solution.py:123
  91.3 17.1 %collective-permute-start.20 = (bf16[2,4,16,2048]{3,2,1,0:T(8,128)(2,1)}, bf16[2,4,16,2048]{3,2,1,0:T(8,128)(2,1)S(1)}, u32[]{:S(2)}, u32[]{:S(2)}) collective-permute-start(bf16[2,4,16,2048]{3,2,1,0:T(8,128)(2,1)} %pad_maximum_fusion.13), channel_id=1, source_target_pairs={{0,16},{16,0},{1,17},{17,1},{2,18},{18,2},{3,19},{19,3},{4,20},{20... | collective-permute-start | bytes 1572872 | tf_op jit(solution)/shard_map/ppermute | solution.py:123
  92.5 18.3 %collective-permute-start.22 = (bf16[2,4,16,2048]{3,2,1,0:T(8,128)(2,1)}, bf16[2,4,16,2048]{3,2,1,0:T(8,128)(2,1)S(1)}, u32[]{:S(2)}, u32[]{:S(2)}) collective-permute-start(bf16[2,4,16,2048]{3,2,1,0:T(8,128)(2,1)} %pad_maximum_fusion.14), channel_id=1, source_target_pairs={{0,2},{1,3},{2,0},{3,1},{4,6},{5,7},{6,4},{7,5},{8,10},{9,11},{10,... | collective-permute-start | bytes 1572872 | tf_op jit(solution)/shard_map/ppermute | solution.py:123
  110.3 3.0 %collective-permute-start.21 = (bf16[2,2,4,16,2048]{4,3,2,0,1:T(8,128)(2,1)}, bf16[2,2,4,16,2048]{4,3,2,0,1:T(8,128)(2,1)}, u32[]{:S(2)}, u32[]{:S(2)}) collective-permute-start(bf16[2,2,4,16,2048]{4,3,2,0,1:T(8,128)(2,1)} %pad_maximum_fusion.3), channel_id=1, source_target_pairs={{0,1},{1,0},{2,3},{3,2},{4,5},{5,4},{6,7},{7,6},{8,9},{9,8},{10,11... | collective-permute-start | bytes 3145736 | tf_op jit(solution)/shard_map/ppermute | solution.py:123
  112.6 3.0 %collective-permute-start.23 = (bf16[2,2,4,16,2048]{4,3,2,0,1:T(8,128)(2,1)}, bf16[2,2,4,16,2048]{4,3,2,0,1:T(8,128)(2,1)}, u32[]{:S(2)}, u32[]{:S(2)}) collective-permute-start(bf16[2,2,4,16,2048]{4,3,2,0,1:T(8,128)(2,1)} %maximum_bitcast_fusion.4), channel_id=1, source_target_pairs={{0,1},{1,0},{2,3},{3,2},{4,5},{5,4},{6,7},{7,6},{8,9},{9,8},{10,11... | collective-permute-start | bytes 3145736 | tf_op jit(solution)/shard_map/ppermute | solution.py:123
  112.8 2.9 %copy-start.15 = (bf16[1,2,4,16,2048]{4,3,2,1,0:T(8,128)(2,1)S(1)}, bf16[1,2,4,16,2048]{4,3,2,1,0:T(8,128)(2,1)}, u32[]{:S(2)}) copy-start(bf16[1,2,4,16,2048]{4,3,2,1,0:T(8,128)(2,1)} %copy-done.14) | copy-start | bytes 1572868
  124.3 3.2 %collective-permute-start.24 = (f32[384,256]{1,0:T(8,128)S(1)}, f32[384,256]{1,0:T(8,128)}, u32[]{:S(2)}, u32[]{:S(2)}) collective-permute-start(f32[384,256]{1,0:T(8,128)S(1)} %dynamic-slice_bitcast_fusion.2), channel_id=1, source_target_pairs={{0,1},{1,0},{2,3},{3,2},{4,5},{5,4},{6,7},{7,6},{8,9},{9,8},{10,11... | collective-permute-start | bytes 1179656 | tf_op jit(solution)/shard_map/ppermute | solution.py:123
  124.5 3.0 %copy-start.3 = (f32[3,256,256]{2,1,0:T(8,128)S(1)}, f32[3,256,256]{2,1,0:T(8,128)}, u32[]{:S(2)}) copy-start(f32[3,256,256]{2,1,0:T(8,128)} %copy-done.2) | copy-start | bytes 2359300
  129.6 7.9 %collective-permute-start.25 = (f32[896,256]{1,0:T(8,128)}, f32[896,256]{1,0:T(8,128)}, u32[]{:S(2)}, u32[]{:S(2)}) collective-permute-start(f32[896,256]{1,0:T(8,128)} %dynamic-slice_bitcast_fusion), channel_id=1, source_target_pairs={{0,1},{1,0},{2,3},{3,2},{4,5},{5,4},{6,7},{7,6},{8,9},{9,8},{10,11... | collective-permute-start | bytes 2752520 | tf_op jit(solution)/shard_map/ppermute | solution.py:123
  130.0 6.5 %collective-permute-start.26 = (f32[192,256]{1,0:T(8,128)S(1)}, f32[192,256]{1,0:T(8,128)}, u32[]{:S(2)}, u32[]{:S(2)}) collective-permute-start(f32[192,256]{1,0:T(8,128)S(1)} %dynamic-slice_bitcast_fusion.4), channel_id=1, source_target_pairs={{0,2},{1,3},{2,0},{3,1},{4,6},{5,7},{6,4},{7,5},{8,10},{9,11},{10,... | collective-permute-start | bytes 589832 | tf_op jit(solution)/shard_map/ppermute | solution.py:123
  138.8 25.3 %copy-start.19 = (s32[512]{0:T(512)S(1)}, s32[512]{0:T(512)}, u32[]{:S(2)}) copy-start(s32[512]{0:T(512)} %param.21) | copy-start | bytes 6148
  138.8 25.3 %copy-start.22 = (s32[64]{0:T(128)S(1)}, s32[64]{0:T(128)}, u32[]{:S(2)}) copy-start(s32[64]{0:T(128)} %param.22) | copy-start | bytes 772
  138.8 18.4 %collective-permute-start.27 = (f32[448,256]{1,0:T(8,128)S(1)}, f32[448,256]{1,0:T(8,128)S(1)}, u32[]{:S(2)}, u32[]{:S(2)}) collective-permute-start(f32[448,256]{1,0:T(8,128)S(1)} %dynamic-slice_bitcast_fusion.1), channel_id=1, source_target_pairs={{0,2},{1,3},{2,0},{3,1},{4,6},{5,7},{6,4},{7,5},{8,10},{9,11},{10,... | collective-permute-start | bytes 1376264 | tf_op jit(solution)/shard_map/ppermute | solution.py:123
  139.1 5.2 %collective-permute-start.28 = (f32[192,256]{1,0:T(8,128)S(1)}, f32[192,256]{1,0:T(8,128)S(1)}, u32[]{:S(2)}, u32[]{:S(2)}) collective-permute-start(f32[192,256]{1,0:T(8,128)S(1)} %bitcast_add_fusion.4), channel_id=1, source_target_pairs={{0,4},{1,5},{2,6},{3,7},{4,0},{5,1},{6,2},{7,3},{8,12},{9,13},{10,... | collective-permute-start | bytes 589832 | tf_op jit(solution)/shard_map/ppermute | solution.py:123
  144.3 12.3 %collective-permute-start.29 = (f32[192,256]{1,0:T(8,128)S(1)}, f32[192,256]{1,0:T(8,128)S(1)}, u32[]{:S(2)}, u32[]{:S(2)}) collective-permute-start(f32[192,256]{1,0:T(8,128)S(1)} %add.168), channel_id=1, source_target_pairs={{0,8},{1,9},{2,10},{3,11},{4,12},{5,13},{6,14},{7,15},{8,0},{9,1},... | collective-permute-start | bytes 589832 | tf_op jit(solution)/shard_map/ppermute | solution.py:123
  156.6 5.1 %collective-permute-start.31 = (f32[192,256]{1,0:T(8,128)S(1)}, f32[192,256]{1,0:T(8,128)S(1)}, u32[]{:S(2)}, u32[]{:S(2)}) collective-permute-start(f32[192,256]{1,0:T(8,128)S(1)} %add.169), channel_id=1, source_target_pairs={{0,2},{1,3},{2,0},{3,1},{4,6},{5,7},{6,4},{7,5},{8,10},{9,11},{10,... | collective-permute-start | bytes 589832 | tf_op jit(solution)/shard_map/ppermute | solution.py:123
  161.8 5.4 %collective-permute-start.32 = (f32[384,256]{1,0:T(8,128)S(1)}, f32[384,256]{1,0:T(8,128)S(1)}, u32[]{:S(2)}, u32[]{:S(2)}) collective-permute-start(f32[384,256]{1,0:T(8,128)S(1)} %bitcast.304), channel_id=1, source_target_pairs={{0,1},{1,0},{2,3},{3,2},{4,5},{5,4},{6,7},{7,6},{8,9},{9,8},{10,11... | collective-permute-start | bytes 1179656 | tf_op jit(solution)/shard_map/ppermute | solution.py:123
  164.5 9.5 %collective-permute-start.30 = (f32[224,256]{1,0:T(8,128)S(1)}, f32[224,256]{1,0:T(8,128)S(1)}, u32[]{:S(2)}, u32[]{:S(2)}) collective-permute-start(f32[224,256]{1,0:T(8,128)S(1)} %dynamic-slice_bitcast_fusion.3), channel_id=1, source_target_pairs={{0,4},{1,5},{2,6},{3,7},{4,0},{5,1},{6,2},{7,3},{8,12},{9,13},{10,... | collective-permute-start | bytes 688136 | tf_op jit(solution)/shard_map/ppermute | solution.py:123
  174.1 8.1 %collective-permute-start.33 = (f32[112,256]{1,0:T(8,128)S(1)}, f32[112,256]{1,0:T(8,128)S(1)}, u32[]{:S(2)}, u32[]{:S(2)}) collective-permute-start(f32[112,256]{1,0:T(8,128)S(1)} %dynamic-slice_bitcast_fusion.8), channel_id=1, source_target_pairs={{0,8},{1,9},{2,10},{3,11},{4,12},{5,13},{6,14},{7,15},{8,0},{9,1},... | collective-permute-start | bytes 344072 | tf_op jit(solution)/shard_map/ppermute | solution.py:123
  182.2 8.3 %collective-permute-start.34 = (f32[112,256]{1,0:T(8,128)S(1)}, f32[112,256]{1,0:T(8,128)S(1)}, u32[]{:S(2)}, u32[]{:S(2)}) collective-permute-start(f32[112,256]{1,0:T(8,128)S(1)} %bitcast_add_fusion.5), channel_id=1, source_target_pairs={{0,8},{1,9},{2,10},{3,11},{4,12},{5,13},{6,14},{7,15},{8,0},{9,1},... | collective-permute-start | bytes 344072 | tf_op jit(solution)/shard_map/ppermute | solution.py:123
  190.6 6.8 %collective-permute-start.35 = (f32[224,256]{1,0:T(8,128)S(1)}, f32[224,256]{1,0:T(8,128)S(1)}, u32[]{:S(2)}, u32[]{:S(2)}) collective-permute-start(f32[224,256]{1,0:T(8,128)S(1)} %bitcast.308), channel_id=1, source_target_pairs={{0,4},{1,5},{2,6},{3,7},{4,0},{5,1},{6,2},{7,3},{8,12},{9,13},{10,... | collective-permute-start | bytes 688136 | tf_op jit(solution)/shard_map/ppermute | solution.py:123
  197.5 10.8 %collective-permute-start.36 = (f32[448,256]{1,0:T(8,128)S(1)}, f32[448,256]{1,0:T(8,128)S(1)}, u32[]{:S(2)}, u32[]{:S(2)}) collective-permute-start(f32[448,256]{1,0:T(8,128)S(1)} %bitcast.303), channel_id=1, source_target_pairs={{0,2},{1,3},{2,0},{3,1},{4,6},{5,7},{6,4},{7,5},{8,10},{9,11},{10,... | collective-permute-start | bytes 1376264 | tf_op jit(solution)/shard_map/ppermute | solution.py:123
  209.4 8.1 %collective-permute-start.37 = (f32[896,256]{1,0:T(8,128)}, f32[896,256]{1,0:T(8,128)}, u32[]{:S(2)}, u32[]{:S(2)}) collective-permute-start(f32[896,256]{1,0:T(8,128)} %bitcast.119), channel_id=1, source_target_pairs={{0,1},{1,0},{2,3},{3,2},{4,5},{5,4},{6,7},{7,6},{8,9},{9,8},{10,11... | collective-permute-start | bytes 2752520 | tf_op jit(solution)/shard_map/ppermute | solution.py:123
  211.6 5.8 %copy-start.20 = (bf16[4,1024]{1,0:T(4,128)(2,1)S(1)}, bf16[4,1024]{1,0:T(4,128)(2,1)}, u32[]{:S(2)}) copy-start(bf16[4,1024]{1,0:T(4,128)(2,1)} %param.23) | copy-start | bytes 24580
  211.6 52.9 %all-to-all-start = ((bf16[16,4,16,1024]{3,2,1,0:T(8,128)(2,1)}), bf16[16,4,16,1024]{3,2,1,0:T(8,128)(2,1)S(1)}, u32[]{:S(2)}, u32[]{:S(2)}) async-start(bf16[16,4,16,1024]{3,2,1,0:T(8,128)(2,1)} %bitcast.299), calls=%async_computation | async-start | bytes 4194304 | tf_op jit(solution)/shard_map/all_to_all | solution.py:555
  219.2 50.8 %copy-start.1 = (bf16[2048,64]{0,1:T(8,128)(2,1)S(1)}, bf16[2048,64]{0,1:T(8,128)(2,1)}, u32[]{:S(2)}) copy-start(bf16[2048,64]{0,1:T(8,128)(2,1)} %param.20) | copy-start | bytes 786436
  (16 other events, 24.5 us)

commit v2 on v1

--- a/solution.py
+++ b/solution.py
@@ -218,6 +218,8 @@
             jnp.where(inside, jnp.where(lane == first + t, 1.0, 0.0), jnp.broadcast_to(panel[t : t + 1, :], shape))
             for t in range(PANEL)
         ]
+        ahead = columns[0] if p + 1 < count else None
+        moved = jnp.where(inside, 0.0, rows[p + 1]) if p + 1 < count else None
         ratio = [[None] * PANEL for _ in range(PANEL)]
         kept = jnp.zeros(shape, jnp.float32)
         solved = [None] * PANEL
@@ -228,16 +230,21 @@
                 ratio[a][t] = entry[a][t] * inverse
             for a in range(t + 1, PANEL):
                 for b in range(t + 1, a + 1):
-                    entry[a][b] = entry[a][b] - ratio[a][t] * entry[b][t]
+                    entry[a][b] = entry[a][b] - (entry[a][t] * entry[b][t]) * inverse
             kept = jnp.where(sub == t, forward[t] * root, kept)
             solved[t] = forward[t] * inverse
+            if ahead is not None:
+                moved = moved - ahead[t] * solved[t]
+                ahead = ahead[: t + 1] + [ahead[a] - ratio[a][t] * ahead[t] for a in range(t + 1, PANEL)]
             for a in range(t + 1, PANEL):
                 forward[a] = forward[a] - ratio[a][t] * forward[t]
         for t in range(PANEL - 1, 0, -1):
             for a in range(t):
                 solved[a] = solved[a] - ratio[t][a] * solved[t]
         result.append(jnp.where(lane <= first + sub, kept, 0.0))
-        for i in range(p + 1, count):
+        if p + 1 < count:
+            rows[p + 1] = moved
+        for i in range(p + 2, count):
             col = columns[i - p - 1]
             terms = [col[t] * solved[t] for t in range(PANEL)]
             while len(terms) > 1:
@@ -342,7 +349,7 @@
     )(*operands)
 
 
-CHAIN_FLOPS = 30_000_000_000
+CHAIN_FLOPS = 10_000_000
 
 
 def inverse_first(tiles, scale, ridge):
@@ -439,11 +446,9 @@
             part = halve(part, bit, (), besides[at : at + 1])
             at += 1
         for bit in bits[::-1]:
+            part = rejoin(part, bit, *besides[at : at + 1])
             if bit == 2:
                 outgoing = after(outgoing, part)
-                part = rejoin(part, bit, outgoing)
-            else:
-                part = rejoin(part, bit, *besides[at : at + 1])
             at += 1
         return part, outgoing
 

time: 274 us -> 273 us (level)
  Pallas kernels: 78.7 us -> 65.4 us
  waiting for transfers between devices: 88.1 us -> 97.7 us
    pallas_call x5, Pallas kernels: 54.2 us -> 41 us  [kernel_call(): pl.pallas_call(kernel, out_shape=out, in_specs=[whole] * len(operands), o...]
    all_to_all x1, waiting for transfers between devices: 15.4 us -> 20.9 us  [body(): lax.all_to_all(outgoing.reshape(device_count, lists_owned, slot_count, mo...]
    ppermute x38, waiting for transfers between devices: 72.7 us -> 76.7 us  [exchange(): lax.ppermute(part, axis, [(i, i ^ bit) for i in range(lax.axis_size(axis))])]
  transfers between devices with their start and end apart: 39 -> 39, of which waited for: 18 -> 22; matrix products, arithmetic and copies ran while one was open for 11% -> 11% of each run, Pallas kernels for 27% -> 22%
where the time goes in v2:
time: 273 us; the launch traced here: 269 us
  waiting for transfers between devices  97.7 us (36%)
  Pallas kernels  65.4 us (24%)
  starting transfers between devices  56.6 us (21%)
  other arithmetic  21.8 us (8%)
  local copies, waits for them, and re-layouts  14.9 us (5%)
  matrix products  11.5 us (4%)
    ppermute x38, waiting for transfers between devices, exchange(): lax.ppermute(part, axis, [(i, i ^ bit) for i in range(lax.axis_size(axis))])  76.7 us
    ppermute x38, starting transfers between devices, exchange(): lax.ppermute(part, axis, [(i, i ^ bit) for i in range(lax.axis_size(axis))])  49.3 us
    pallas_call x5, Pallas kernels, kernel_call(): pl.pallas_call(kernel, out_shape=out, in_specs=[whole] * len(operands), o...  41 us
    all_to_all x1, waiting for transfers between devices, body(): lax.all_to_all(outgoing.reshape(device_count, lists_owned, slot_count, mo...  20.9 us
    pallas_call x1, Pallas kernels, attend(): pl.pallas_call(functools.partial(attend_kernel, head_dim), grid=(steps,),...  9.11 us
    another operation x43, other arithmetic, ordered(): return jnp.stack([jnp.where(low, part, other), jnp.where(low, other, part)])  8.56 us
    unnamed x51, local copies, waits for them, and re-layouts  7.72 us
    all_to_all x1, starting transfers between devices, body(): lax.all_to_all(outgoing.reshape(device_count, lists_owned, slot_count, mo...  7.22 us
  transfers between devices with their start and end apart: 39, of which 22 were waited for; matrix products, arithmetic and copies ran while one was open for 11% of the time, Pallas kernels for 22%

profile of v2, /device:TPU:13, one launch (start us, length us, event | category | flops | bytes accessed | tf_op | source)
XLA Modules:
  0.0 268.9 jit_solution(12352548029545547133)
XLA Ops:
  1.0 2.4 collective-permute-start
  4.5 7.6 %collective-permute-done = bf16[2,48,1024]{2,1,0:T(8,128)(2,1)S(1)} collective-permute-done((bf16[2,48,1024]{2,1,0:T(8,128)(2,1)S(1)}, bf16[2,48,1024]{2,1,0:T(8,128)(2,1)S(1)}, u32[]{:S(2)}, u32[]{:S(2)}) %collective-permute-start) | collective-permute-done | bytes 196640 | tf_op jit(solution)/shard_map/ppermute | solution.py:123
  13.5 9.8 %collective-permute-done.1 = bf16[2,2,48,1024]{3,2,1,0:T(8,128)(2,1)S(1)} collective-permute-done((bf16[2,2,48,1024]{3,2,1,0:T(8,128)(2,1)S(1)}, bf16[2,2,48,1024]{3,2,1,0:T(8,128)(2,1)S(1)}, u32[]{:S(2)}, u32[]{:S(2)}) %collective-permute-start.1) | collective-permute-done | bytes 393248 | tf_op jit(solution)/shard_map/ppermute | solution.py:123
  23.5 3.2 %collective-permute-start.8 = (bf16[2,48,1024]{2,1,0:T(8,128)(2,1)S(1)}, bf16[2,48,1024]{2,1,0:T(8,128)(2,1)S(1)}, u32[]{:S(2)}, u32[]{:S(2)}) collective-permute-start(bf16[2,48,1024]{2,1,0:T(8,128)(2,1)S(1)} %dynamic-slice_bitcast_fusion.5), channel_id=1, source_target_pairs={{0,8},{1,9},{2,10},{3,11},{4,12},{5,13},{6,14},{7,15},{8,0},{9,1},... | collective-permute-start | bytes 589832 | tf_op jit(solution)/shard_map/ppermute | solution.py:123
  28.5 7.0 %collective-permute-done.8 = bf16[2,48,1024]{2,1,0:T(8,128)(2,1)S(1)} collective-permute-done((bf16[2,48,1024]{2,1,0:T(8,128)(2,1)S(1)}, bf16[2,48,1024]{2,1,0:T(8,128)(2,1)S(1)}, u32[]{:S(2)}, u32[]{:S(2)}) %collective-permute-start.8) | collective-permute-done | bytes 196640 | tf_op jit(solution)/shard_map/ppermute | solution.py:123
  38.6 7.2 %collective-permute-done.9 = bf16[2,2,48,1024]{3,2,1,0:T(8,128)(2,1)S(1)} collective-permute-done((bf16[2,2,48,1024]{3,2,1,0:T(8,128)(2,1)S(1)}, bf16[2,2,48,1024]{3,2,1,0:T(8,128)(2,1)S(1)}, u32[]{:S(2)}, u32[]{:S(2)}) %collective-permute-start.9) | collective-permute-done | bytes 393248 | tf_op jit(solution)/shard_map/ppermute | solution.py:123
  45.9 3.2 %collective-permute-start.16 = (bf16[2,16,2048]{2,1,0:T(8,128)(2,1)S(1)}, bf16[2,16,2048]{2,1,0:T(8,128)(2,1)S(1)}, u32[]{:S(2)}, u32[]{:S(2)}) collective-permute-start(bf16[2,16,2048]{2,1,0:T(8,128)(2,1)S(1)} %dynamic-slice_bitcast_fusion.7), channel_id=1, source_target_pairs={{0,8},{1,9},{2,10},{3,11},{4,12},{5,13},{6,14},{7,15},{8,0},{9,1},... | collective-permute-start | bytes 393224 | tf_op jit(solution)/shard_map/ppermute | solution.py:123
  50.6 4.4 %collective-permute-done.16 = bf16[2,16,2048]{2,1,0:T(8,128)(2,1)S(1)} collective-permute-done((bf16[2,16,2048]{2,1,0:T(8,128)(2,1)S(1)}, bf16[2,16,2048]{2,1,0:T(8,128)(2,1)S(1)}, u32[]{:S(2)}, u32[]{:S(2)}) %collective-permute-start.16) | collective-permute-done | bytes 131104 | tf_op jit(solution)/shard_map/ppermute | solution.py:123
  55.7 4.0 %collective-permute-start.4 = (bf16[2,2,4,48,1024]{4,3,2,1,0:T(8,128)(2,1)S(1)}, bf16[2,2,4,48,1024]{4,3,2,1,0:T(8,128)(2,1)S(1)}, u32[]{:S(2)}, u32[]{:S(2)}) collective-permute-start(bf16[2,2,4,48,1024]{4,3,2,1,0:T(8,128)(2,1)S(1)} %pad_maximum_fusion.1), channel_id=1, source_target_pairs={{0,1},{1,0},{2,3},{3,2},{4,5},{5,4},{6,7},{7,6},{8,9},{9,8},{10,11... | collective-permute-start | bytes 4718600 | tf_op jit(solution)/shard_map/ppermute | solution.py:123
  59.9 1.4 collective-permute-start.7
  68.6 5.0 %convolution_convert_fusion.query_ref.key_ref.value_ref = bf16[3072,512]{1,0:T(8,128)(2,1)S(1)} fusion(bf16[3072,1024]{1,0:T(8,128)(2,1)S(1)} %bitcast.283, bf16[512,1024]{1,0:T(8,128)(2,1)} %param.14), kind=kOutput, calls=%fused_computation.2 | convolution fusion | flops 3222798336 | bytes 10485760 | tf_op jit(solution)/shard_map/dot_general | solution.py:529
  73.7 9.1 %shard_map.136 = bf16[1024,512]{1,0:T(8,128)(2,1)S(1)} custom-call(s32[512,1]{1,0:T(8,128)S(1)} %copy.85.column_ref, s32[1,512]{1,0:T(1,128)S(1)} %bitcast.272, bf16[3072,512]{1,0:T(8,128)(2,1)S(1)} %convolution_convert_fusion.query_ref.key_ref.value_ref, bf16[3072,512]{1,0:T(8,128)(2,1)S(1)} %convolution_convert_fusion.query_ref.key_ref.value_ref, ...), custom_call_target="tpu_custom_call" | custom-call | flops 1073741824 | bytes 4194304 | tf_op jit(solution)/shard_map/pallas_call | solution.py:57
  84.0 2.0 collective-permute-done.18
  86.3 3.7 %collective-permute-start.13 = (bf16[2,2,4,48,1024]{4,3,2,0,1:T(8,128)(2,1)S(1)}, bf16[2,2,4,48,1024]{4,3,2,0,1:T(8,128)(2,1)S(1)}, u32[]{:S(2)}, u32[]{:S(2)}) collective-permute-start(bf16[2,2,4,48,1024]{4,3,2,0,1:T(8,128)(2,1)S(1)} %pad_maximum_fusion.2), channel_id=1, source_target_pairs={{0,1},{1,0},{2,3},{3,2},{4,5},{5,4},{6,7},{7,6},{8,9},{9,8},{10,11... | collective-permute-start | bytes 4718600 | tf_op jit(solution)/shard_map/ppermute | solution.py:123
  93.6 1.7 collective-permute-done.15
  99.2 1.4 fusion.3
  101.6 6.7 %shard_map.137 = bf16[512,2048]{1,0:T(8,128)(2,1)S(1)} custom-call(bf16[512,1024]{1,0:T(8,128)(2,1)S(1)} %multiply_convert_fusion.1.rows_ref, bf16[2048,1024]{1,0:T(8,128)(2,1)S(1)} %bitcast.267), custom_call_target="tpu_custom_call" | custom-call | flops 8589934592 | bytes 8388608 | tf_op jit(solution)/shard_map/pallas_call | solution.py:106
  113.4 1.7 broadcast_select_fusion.11
  115.7 1.4 broadcast_select_fusion.9
  118.5 2.5 fusion.4
  122.0 1.6 shard_map.138
  124.7 3.0 %shard_map.139 = f32[7,256,256]{2,1,0:T(8,128)S(1)} custom-call(s32[7]{0:T(128)S(1)} %copy-done.6, s32[7]{0:T(128)S(1)} %copy-done.7, bf16[512,1024]{1,0:T(8,128)(2,1)S(1)} %multiply_convert_fusion.left_ref.right_ref, bf16[512,1024]{1,0:T(8,128)(2,1)S(1)} %multiply_convert_fusion.left_ref.right_ref), custom_call_target="tpu_custom_call" | custom-call | flops 469762048 | bytes 4194304 | tf_op jit(solution)/shard_map/pallas_call | solution.py:396
  130.5 6.2 %collective-permute-done.26 = f32[192,256]{1,0:T(8,128)} collective-permute-done((f32[192,256]{1,0:T(8,128)S(1)}, f32[192,256]{1,0:T(8,128)}, u32[]{:S(2)}, u32[]{:S(2)}) %collective-permute-start.26) | collective-permute-done | bytes 196640 | tf_op jit(solution)/shard_map/ppermute | solution.py:123
  137.7 1.3 bitcast_add_fusion
  139.4 1.3 collective-permute-start.28
  140.7 3.9 %collective-permute-done.28 = f32[192,256]{1,0:T(8,128)S(1)} collective-permute-done((f32[192,256]{1,0:T(8,128)S(1)}, f32[192,256]{1,0:T(8,128)S(1)}, u32[]{:S(2)}, u32[]{:S(2)}) %collective-permute-start.28) | collective-permute-done | bytes 196640 | tf_op jit(solution)/shard_map/ppermute | solution.py:123
  144.5 4.3 %collective-permute-start.29 = (f32[192,256]{1,0:T(8,128)S(1)}, f32[192,256]{1,0:T(8,128)S(1)}, u32[]{:S(2)}, u32[]{:S(2)}) collective-permute-start(f32[192,256]{1,0:T(8,128)S(1)} %add.168), channel_id=1, source_target_pairs={{0,8},{1,9},{2,10},{3,11},{4,12},{5,13},{6,14},{7,15},{8,0},{9,1},... | collective-permute-start | bytes 589832 | tf_op jit(solution)/shard_map/ppermute | solution.py:123
  148.9 7.9 %collective-permute-done.29 = f32[192,256]{1,0:T(8,128)S(1)} collective-permute-done((f32[192,256]{1,0:T(8,128)S(1)}, f32[192,256]{1,0:T(8,128)S(1)}, u32[]{:S(2)}, u32[]{:S(2)}) %collective-permute-start.29) | collective-permute-done | bytes 196640 | tf_op jit(solution)/shard_map/ppermute | solution.py:123
  157.6 4.3 %collective-permute-done.31 = f32[192,256]{1,0:T(8,128)S(1)} collective-permute-done((f32[192,256]{1,0:T(8,128)S(1)}, f32[192,256]{1,0:T(8,128)S(1)}, u32[]{:S(2)}, u32[]{:S(2)}) %collective-permute-start.31) | collective-permute-done | bytes 196640 | tf_op jit(solution)/shard_map/ppermute | solution.py:123
  161.9 2.4 collective-permute-start.32
  164.3 2.7 %collective-permute-start.30 = (f32[224,256]{1,0:T(8,128)S(1)}, f32[224,256]{1,0:T(8,128)S(1)}, u32[]{:S(2)}, u32[]{:S(2)}) collective-permute-start(f32[224,256]{1,0:T(8,128)S(1)} %dynamic-slice_bitcast_fusion.3), channel_id=1, source_target_pairs={{0,4},{1,5},{2,6},{3,7},{4,0},{5,1},{6,2},{7,3},{8,12},{9,13},{10,... | collective-permute-start | bytes 688136 | tf_op jit(solution)/shard_map/ppermute | solution.py:123
  167.2 5.2 %shard_map.140.work_ref = f32[512,512]{1,0:T(8,128)S(1)} custom-call(f32[3,256,256]{2,1,0:T(8,128)S(1)} %bitcast.268), custom_call_target="tpu_custom_call" | custom-call | flops 2500000 | bytes 4194304 | tf_op jit(solution)/shard_map/pallas_call | solution.py:341
  173.0 1.8 collective-permute-start.33
  174.8 5.1 %shard_map.141.work_ref = f32[512,512]{1,0:T(8,128)S(1)} custom-call(f32[512,512]{1,0:T(8,128)S(1)} %shard_map.140.work_ref), custom_call_target="tpu_custom_call" | custom-call | flops 2500000 | bytes 4194304 | tf_op jit(solution)/shard_map/pallas_call | solution.py:341
  180.1 3.2 %collective-permute-start.34 = (f32[112,256]{1,0:T(8,128)S(1)}, f32[112,256]{1,0:T(8,128)S(1)}, u32[]{:S(2)}, u32[]{:S(2)}) collective-permute-start(f32[112,256]{1,0:T(8,128)S(1)} %bitcast_add_fusion.5), channel_id=1, source_target_pairs={{0,8},{1,9},{2,10},{3,11},{4,12},{5,13},{6,14},{7,15},{8,0},{9,1},... | collective-permute-start | bytes 344072 | tf_op jit(solution)/shard_map/ppermute | solution.py:123
  183.3 5.1 %shard_map.142.work_ref = f32[512,512]{1,0:T(8,128)S(1)} custom-call(f32[512,512]{1,0:T(8,128)S(1)} %shard_map.141.work_ref), custom_call_target="tpu_custom_call" | custom-call | flops 2500000 | bytes 4194304 | tf_op jit(solution)/shard_map/pallas_call | solution.py:341
  188.4 2.2 collective-permute-start.35
  191.0 4.6 %shard_map.143.first_ref = f32[512,512]{1,0:T(8,128)S(1)} custom-call(f32[512,512]{1,0:T(8,128)S(1)} %shard_map.142.work_ref), custom_call_target="tpu_custom_call" | custom-call | flops 2500000 | bytes 4194304 | tf_op jit(solution)/shard_map/pallas_call | solution.py:341
  197.3 2.6 select_convert_fusion
  199.9 7.5 %collective-permute-done.36 = f32[448,256]{1,0:T(8,128)S(1)} collective-permute-done((f32[448,256]{1,0:T(8,128)S(1)}, f32[448,256]{1,0:T(8,128)S(1)}, u32[]{:S(2)}, u32[]{:S(2)}) %collective-permute-start.36) | collective-permute-done | bytes 458784 | tf_op jit(solution)/shard_map/ppermute | solution.py:123
  208.4 7.2 %all-to-all-start = ((bf16[16,4,16,1024]{3,2,1,0:T(8,128)(2,1)}), bf16[16,4,16,1024]{3,2,1,0:T(8,128)(2,1)S(1)}, u32[]{:S(2)}, u32[]{:S(2)}) async-start(bf16[16,4,16,1024]{3,2,1,0:T(8,128)(2,1)} %bitcast.300), calls=%async_computation | async-start | bytes 4194304 | tf_op jit(solution)/shard_map/all_to_all | solution.py:560
  216.0 2.3 collective-permute-done.37
  218.4 1.3 select_bitcast_fusion.1
  219.8 21.0 %shard_map.144.inverse_ref = bf16[1024,1024]{1,0:T(8,128)(2,1)S(1)} custom-call(f32[512,512]{1,0:T(8,128)S(1)} %shard_map.143.first_ref, f32[7,256,256]{2,1,0:T(8,128)S(1)} %bitcast.266), custom_call_target="tpu_custom_call" | custom-call | flops 10000000 | bytes 4194304 | tf_op jit(solution)/shard_map/pallas_call | solution.py:341
  240.8 1.3 copy-done.2
  242.1 20.9 %all-to-all-done.rows_ref = bf16[16,4,16,1024]{3,2,1,0:T(8,128)(2,1)S(1)} async-done(((bf16[16,4,16,1024]{3,2,1,0:T(8,128)(2,1)}), bf16[16,4,16,1024]{3,2,1,0:T(8,128)(2,1)S(1)}, u32[]{:S(2)}, u32[]{:S(2)}) %all-to-all-start) | async-done | bytes 2097184 | tf_op jit(solution)/shard_map/all_to_all | solution.py:560
  263.1 1.6 copy-done.3
  264.7 4.0 %shard_map.145 = bf16[4,256,1024]{2,1,0:T(8,128)(2,1)} custom-call(bf16[16,4,16,1024]{3,2,1,0:T(8,128)(2,1)S(1)} %all-to-all-done.rows_ref, bf16[1024,1024]{1,0:T(8,128)(2,1)S(1)} %copy-done.3, bf16[4,1,1024]{2,1,0:T(2,128)(2,1)S(1)} %copy.98.centroids_ref), custom_call_target="tpu_custom_call" | custom-call | tf_op jit(solution)/shard_map/pallas_call | solution.py:468
  (196 shorter events, 46.7 us)
Async XLA Ops:
  0.0 13.5 %copy-start = (bf16[2048,64]{0,1:T(8,128)(2,1)S(1)}, bf16[2048,64]{0,1:T(8,128)(2,1)}, u32[]{:S(2)}) copy-start(bf16[2048,64]{0,1:T(8,128)(2,1)} %param.20) | copy-start | bytes 786436
  0.0 13.2 %copy-start.18 = (bf16[1024,64]{0,1:T(8,128)(2,1)S(1)}, bf16[1024,64]{0,1:T(8,128)(2,1)}, u32[]{:S(2)}) copy-start(bf16[1024,64]{0,1:T(8,128)(2,1)} %param.17) | copy-start | bytes 393220
  0.0 13.3 %copy-start.24 = (s32[1,8]{1,0:T(1,128)S(1)}, s32[1,8]{1,0:T(1,128)}, u32[]{:S(2)}) copy-start(s32[1,8]{1,0:T(1,128)} %param.15) | copy-start | bytes 100
  1.0 11.1 %collective-permute-start = (bf16[2,48,1024]{2,1,0:T(8,128)(2,1)S(1)}, bf16[2,48,1024]{2,1,0:T(8,128)(2,1)S(1)}, u32[]{:S(2)}, u32[]{:S(2)}) collective-permute-start(bf16[2,48,1024]{2,1,0:T(8,128)(2,1)S(1)} %dynamic-slice_bitcast_fusion.6), channel_id=1, source_target_pairs={{0,8},{1,9},{2,10},{3,11},{4,12},{5,13},{6,14},{7,15},{8,0},{9,1},... | collective-permute-start | bytes 589832 | tf_op jit(solution)/shard_map/ppermute | solution.py:123
  13.1 10.3 %collective-permute-start.1 = (bf16[2,2,48,1024]{3,2,1,0:T(8,128)(2,1)S(1)}, bf16[2,2,48,1024]{3,2,1,0:T(8,128)(2,1)S(1)}, u32[]{:S(2)}, u32[]{:S(2)}) collective-permute-start(bf16[2,2,48,1024]{3,2,1,0:T(8,128)(2,1)S(1)} %pad_maximum_fusion.16), channel_id=1, source_target_pairs={{0,4},{1,5},{2,6},{3,7},{4,0},{5,1},{6,2},{7,3},{8,12},{9,13},{10,... | collective-permute-start | bytes 1179656 | tf_op jit(solution)/shard_map/ppermute | solution.py:123
  23.5 12.0 %collective-permute-start.8 = (bf16[2,48,1024]{2,1,0:T(8,128)(2,1)S(1)}, bf16[2,48,1024]{2,1,0:T(8,128)(2,1)S(1)}, u32[]{:S(2)}, u32[]{:S(2)}) collective-permute-start(bf16[2,48,1024]{2,1,0:T(8,128)(2,1)S(1)} %dynamic-slice_bitcast_fusion.5), channel_id=1, source_target_pairs={{0,8},{1,9},{2,10},{3,11},{4,12},{5,13},{6,14},{7,15},{8,0},{9,1},... | collective-permute-start | bytes 589832 | tf_op jit(solution)/shard_map/ppermute | solution.py:123
  26.7 9.1 %collective-permute-start.2 = (bf16[4,48,1024]{2,1,0:T(8,128)(2,1)S(1)}, bf16[4,48,1024]{2,1,0:T(8,128)(2,1)S(1)}, u32[]{:S(2)}, u32[]{:S(2)}) collective-permute-start(bf16[4,48,1024]{2,1,0:T(8,128)(2,1)S(1)} %get-tuple-element.107), channel_id=1, source_target_pairs={{0,2},{1,3},{2,0},{3,1},{4,6},{5,7},{6,4},{7,5},{8,10},{9,11},{10,... | collective-permute-start | bytes 1179656 | tf_op jit(solution)/shard_map/ppermute | solution.py:123
  27.0 8.8 %collective-permute-start.5 = (bf16[4,48,1024]{2,1,0:T(8,128)(2,1)S(1)}, bf16[4,48,1024]{2,1,0:T(8,128)(2,1)S(1)}, u32[]{:S(2)}, u32[]{:S(2)}) collective-permute-start(bf16[4,48,1024]{2,1,0:T(8,128)(2,1)S(1)} %get-tuple-element.108), channel_id=1, source_target_pairs={{0,16},{16,0},{1,17},{17,1},{2,18},{18,2},{3,19},{19,3},{4,20},{20... | collective-permute-start | bytes 1179656 | tf_op jit(solution)/shard_map/ppermute | solution.py:123
  35.6 10.2 %collective-permute-start.9 = (bf16[2,2,48,1024]{3,2,1,0:T(8,128)(2,1)S(1)}, bf16[2,2,48,1024]{3,2,1,0:T(8,128)(2,1)S(1)}, u32[]{:S(2)}, u32[]{:S(2)}) collective-permute-start(bf16[2,2,48,1024]{3,2,1,0:T(8,128)(2,1)S(1)} %pad_maximum_fusion.18), channel_id=1, source_target_pairs={{0,4},{1,5},{2,6},{3,7},{4,0},{5,1},{6,2},{7,3},{8,12},{9,13},{10,... | collective-permute-start | bytes 1179656 | tf_op jit(solution)/shard_map/ppermute | solution.py:123
  36.0 19.4 %collective-permute-start.3 = (bf16[2,4,48,1024]{3,2,1,0:T(8,128)(2,1)S(1)}, bf16[2,4,48,1024]{3,2,1,0:T(8,128)(2,1)S(1)}, u32[]{:S(2)}, u32[]{:S(2)}) collective-permute-start(bf16[2,4,48,1024]{3,2,1,0:T(8,128)(2,1)S(1)} %pad_maximum_fusion.6), channel_id=1, source_target_pairs={{0,16},{16,0},{1,17},{17,1},{2,18},{18,2},{3,19},{19,3},{4,20},{20... | collective-permute-start | bytes 2359304 | tf_op jit(solution)/shard_map/ppermute | solution.py:123
  37.4 22.2 %collective-permute-start.6 = (bf16[2,4,48,1024]{3,2,1,0:T(8,128)(2,1)S(1)}, bf16[2,4,48,1024]{3,2,1,0:T(8,128)(2,1)S(1)}, u32[]{:S(2)}, u32[]{:S(2)}) collective-permute-start(bf16[2,4,48,1024]{3,2,1,0:T(8,128)(2,1)S(1)} %pad_maximum_fusion.7), channel_id=1, source_target_pairs={{0,2},{1,3},{2,0},{3,1},{4,6},{5,7},{6,4},{7,5},{8,10},{9,11},{10,... | collective-permute-start | bytes 2359304 | tf_op jit(solution)/shard_map/ppermute | solution.py:123
  45.9 9.1 %collective-permute-start.16 = (bf16[2,16,2048]{2,1,0:T(8,128)(2,1)S(1)}, bf16[2,16,2048]{2,1,0:T(8,128)(2,1)S(1)}, u32[]{:S(2)}, u32[]{:S(2)}) collective-permute-start(bf16[2,16,2048]{2,1,0:T(8,128)(2,1)S(1)} %dynamic-slice_bitcast_fusion.7), channel_id=1, source_target_pairs={{0,8},{1,9},{2,10},{3,11},{4,12},{5,13},{6,14},{7,15},{8,0},{9,1},... | collective-permute-start | bytes 393224 | tf_op jit(solution)/shard_map/ppermute | solution.py:123
  49.1 13.3 %collective-permute-start.10 = (bf16[4,48,1024]{2,1,0:T(8,128)(2,1)S(1)}, bf16[4,48,1024]{2,1,0:T(8,128)(2,1)S(1)}, u32[]{:S(2)}, u32[]{:S(2)}) collective-permute-start(bf16[4,48,1024]{2,1,0:T(8,128)(2,1)S(1)} %get-tuple-element.102), channel_id=1, source_target_pairs={{0,2},{1,3},{2,0},{3,1},{4,6},{5,7},{6,4},{7,5},{8,10},{9,11},{10,... | collective-permute-start | bytes 1179656 | tf_op jit(solution)/shard_map/ppermute | solution.py:123
  49.4 13.0 %collective-permute-start.11 = (bf16[4,48,1024]{2,1,0:T(8,128)(2,1)S(1)}, bf16[4,48,1024]{2,1,0:T(8,128)(2,1)S(1)}, u32[]{:S(2)}, u32[]{:S(2)}) collective-permute-start(bf16[4,48,1024]{2,1,0:T(8,128)(2,1)S(1)} %get-tuple-element.101), channel_id=1, source_target_pairs={{0,16},{16,0},{1,17},{17,1},{2,18},{18,2},{3,19},{19,3},{4,20},{20... | collective-permute-start | bytes 1179656 | tf_op jit(solution)/shard_map/ppermute | solution.py:123
  55.1 7.4 %collective-permute-start.17 = (bf16[2,2,16,2048]{3,2,1,0:T(8,128)(2,1)S(1)}, bf16[2,2,16,2048]{3,2,1,0:T(8,128)(2,1)S(1)}, u32[]{:S(2)}, u32[]{:S(2)}) collective-permute-start(bf16[2,2,16,2048]{3,2,1,0:T(8,128)(2,1)S(1)} %pad_maximum_fusion.20), channel_id=1, source_target_pairs={{0,4},{1,5},{2,6},{3,7},{4,0},{5,1},{6,2},{7,3},{8,12},{9,13},{10,... | collective-permute-start | bytes 786440 | tf_op jit(solution)/shard_map/ppermute | solution.py:123
  55.7 9.4 %collective-permute-start.4 = (bf16[2,2,4,48,1024]{4,3,2,1,0:T(8,128)(2,1)S(1)}, bf16[2,2,4,48,1024]{4,3,2,1,0:T(8,128)(2,1)S(1)}, u32[]{:S(2)}, u32[]{:S(2)}) collective-permute-start(bf16[2,2,4,48,1024]{4,3,2,1,0:T(8,128)(2,1)S(1)} %pad_maximum_fusion.1), channel_id=1, source_target_pairs={{0,1},{1,0},{2,3},{3,2},{4,5},{5,4},{6,7},{7,6},{8,9},{9,8},{10,11... | collective-permute-start | bytes 4718600 | tf_op jit(solution)/shard_map/ppermute | solution.py:123
  59.9 6.2 %collective-permute-start.7 = (bf16[2,2,4,48,1024]{4,3,2,1,0:T(8,128)(2,1)S(1)}, bf16[2,2,4,48,1024]{4,3,2,1,0:T(8,128)(2,1)S(1)}, u32[]{:S(2)}, u32[]{:S(2)}) collective-permute-start(bf16[2,2,4,48,1024]{4,3,2,1,0:T(8,128)(2,1)S(1)} %maximum_bitcast_fusion.2), channel_id=1, source_target_pairs={{0,1},{1,0},{2,3},{3,2},{4,5},{5,4},{6,7},{7,6},{8,9},{9,8},{10,11... | collective-permute-start | bytes 4718600 | tf_op jit(solution)/shard_map/ppermute | solution.py:123
  62.6 23.4 %collective-permute-start.12 = (bf16[2,4,48,1024]{3,2,1,0:T(8,128)(2,1)S(1)}, bf16[2,4,48,1024]{3,2,1,0:T(8,128)(2,1)S(1)}, u32[]{:S(2)}, u32[]{:S(2)}) collective-permute-start(bf16[2,4,48,1024]{3,2,1,0:T(8,128)(2,1)S(1)} %pad_maximum_fusion.9), channel_id=1, source_target_pairs={{0,16},{16,0},{1,17},{17,1},{2,18},{18,2},{3,19},{19,3},{4,20},{20... | collective-permute-start | bytes 2359304 | tf_op jit(solution)/shard_map/ppermute | solution.py:123
  64.0 26.0 %collective-permute-start.14 = (bf16[2,4,48,1024]{3,2,1,0:T(8,128)(2,1)S(1)}, bf16[2,4,48,1024]{3,2,1,0:T(8,128)(2,1)S(1)}, u32[]{:S(2)}, u32[]{:S(2)}) collective-permute-start(bf16[2,4,48,1024]{3,2,1,0:T(8,128)(2,1)S(1)} %pad_maximum_fusion.10), channel_id=1, source_target_pairs={{0,2},{1,3},{2,0},{3,1},{4,6},{5,7},{6,4},{7,5},{8,10},{9,11},{10,... | collective-permute-start | bytes 2359304 | tf_op jit(solution)/shard_map/ppermute | solution.py:123
  64.4 19.5 %collective-permute-start.19 = (bf16[4,16,2048]{2,1,0:T(8,128)(2,1)S(1)}, bf16[4,16,2048]{2,1,0:T(8,128)(2,1)S(1)}, u32[]{:S(2)}, u32[]{:S(2)}) collective-permute-start(bf16[4,16,2048]{2,1,0:T(8,128)(2,1)S(1)} %slice_bitcast_fusion.5), channel_id=1, source_target_pairs={{0,16},{16,0},{1,17},{17,1},{2,18},{18,2},{3,19},{19,3},{4,20},{20... | collective-permute-start | bytes 786440 | tf_op jit(solution)/shard_map/ppermute | solution.py:123
  65.1 20.9 %collective-permute-start.18 = (bf16[4,16,2048]{2,1,0:T(8,128)(2,1)S(1)}, bf16[4,16,2048]{2,1,0:T(8,128)(2,1)S(1)}, u32[]{:S(2)}, u32[]{:S(2)}) collective-permute-start(bf16[4,16,2048]{2,1,0:T(8,128)(2,1)S(1)} %slice_bitcast_fusion.4), channel_id=1, source_target_pairs={{0,2},{1,3},{2,0},{3,1},{4,6},{5,7},{6,4},{7,5},{8,10},{9,11},{10,... | collective-permute-start | bytes 786440 | tf_op jit(solution)/shard_map/ppermute | solution.py:123
  86.3 6.7 %collective-permute-start.13 = (bf16[2,2,4,48,1024]{4,3,2,0,1:T(8,128)(2,1)S(1)}, bf16[2,2,4,48,1024]{4,3,2,0,1:T(8,128)(2,1)S(1)}, u32[]{:S(2)}, u32[]{:S(2)}) collective-permute-start(bf16[2,2,4,48,1024]{4,3,2,0,1:T(8,128)(2,1)S(1)} %pad_maximum_fusion.2), channel_id=1, source_target_pairs={{0,1},{1,0},{2,3},{3,2},{4,5},{5,4},{6,7},{7,6},{8,9},{9,8},{10,11... | collective-permute-start | bytes 4718600 | tf_op jit(solution)/shard_map/ppermute | solution.py:123
  90.3 5.0 %collective-permute-start.15 = (bf16[2,2,4,48,1024]{4,3,2,0,1:T(8,128)(2,1)S(1)}, bf16[2,2,4,48,1024]{4,3,2,0,1:T(8,128)(2,1)S(1)}, u32[]{:S(2)}, u32[]{:S(2)}) collective-permute-start(bf16[2,2,4,48,1024]{4,3,2,0,1:T(8,128)(2,1)S(1)} %maximum_bitcast_fusion.3), channel_id=1, source_target_pairs={{0,1},{1,0},{2,3},{3,2},{4,5},{5,4},{6,7},{7,6},{8,9},{9,8},{10,11... | collective-permute-start | bytes 4718600 | tf_op jit(solution)/shard_map/ppermute | solution.py:123
  91.3 17.1 %collective-permute-start.20 = (bf16[2,4,16,2048]{3,2,1,0:T(8,128)(2,1)}, bf16[2,4,16,2048]{3,2,1,0:T(8,128)(2,1)S(1)}, u32[]{:S(2)}, u32[]{:S(2)}) collective-permute-start(bf16[2,4,16,2048]{3,2,1,0:T(8,128)(2,1)} %pad_maximum_fusion.13), channel_id=1, source_target_pairs={{0,16},{16,0},{1,17},{17,1},{2,18},{18,2},{3,19},{19,3},{4,20},{20... | collective-permute-start | bytes 1572872 | tf_op jit(solution)/shard_map/ppermute | solution.py:123
  92.5 18.3 %collective-permute-start.22 = (bf16[2,4,16,2048]{3,2,1,0:T(8,128)(2,1)}, bf16[2,4,16,2048]{3,2,1,0:T(8,128)(2,1)S(1)}, u32[]{:S(2)}, u32[]{:S(2)}) collective-permute-start(bf16[2,4,16,2048]{3,2,1,0:T(8,128)(2,1)} %pad_maximum_fusion.14), channel_id=1, source_target_pairs={{0,2},{1,3},{2,0},{3,1},{4,6},{5,7},{6,4},{7,5},{8,10},{9,11},{10,... | collective-permute-start | bytes 1572872 | tf_op jit(solution)/shard_map/ppermute | solution.py:123
  110.4 3.0 %collective-permute-start.21 = (bf16[2,2,4,16,2048]{4,3,2,0,1:T(8,128)(2,1)}, bf16[2,2,4,16,2048]{4,3,2,0,1:T(8,128)(2,1)}, u32[]{:S(2)}, u32[]{:S(2)}) collective-permute-start(bf16[2,2,4,16,2048]{4,3,2,0,1:T(8,128)(2,1)} %pad_maximum_fusion.3), channel_id=1, source_target_pairs={{0,1},{1,0},{2,3},{3,2},{4,5},{5,4},{6,7},{7,6},{8,9},{9,8},{10,11... | collective-permute-start | bytes 3145736 | tf_op jit(solution)/shard_map/ppermute | solution.py:123
  112.7 3.0 %collective-permute-start.23 = (bf16[2,2,4,16,2048]{4,3,2,0,1:T(8,128)(2,1)}, bf16[2,2,4,16,2048]{4,3,2,0,1:T(8,128)(2,1)}, u32[]{:S(2)}, u32[]{:S(2)}) collective-permute-start(bf16[2,2,4,16,2048]{4,3,2,0,1:T(8,128)(2,1)} %maximum_bitcast_fusion.4), channel_id=1, source_target_pairs={{0,1},{1,0},{2,3},{3,2},{4,5},{5,4},{6,7},{7,6},{8,9},{9,8},{10,11... | collective-permute-start | bytes 3145736 | tf_op jit(solution)/shard_map/ppermute | solution.py:123
  112.8 2.9 %copy-start.15 = (bf16[1,2,4,16,2048]{4,3,2,1,0:T(8,128)(2,1)S(1)}, bf16[1,2,4,16,2048]{4,3,2,1,0:T(8,128)(2,1)}, u32[]{:S(2)}) copy-start(bf16[1,2,4,16,2048]{4,3,2,1,0:T(8,128)(2,1)} %copy-done.14) | copy-start | bytes 1572868
  124.5 3.2 %collective-permute-start.24 = (f32[384,256]{1,0:T(8,128)S(1)}, f32[384,256]{1,0:T(8,128)}, u32[]{:S(2)}, u32[]{:S(2)}) collective-permute-start(f32[384,256]{1,0:T(8,128)S(1)} %dynamic-slice_bitcast_fusion.2), channel_id=1, source_target_pairs={{0,1},{1,0},{2,3},{3,2},{4,5},{5,4},{6,7},{7,6},{8,9},{9,8},{10,11... | collective-permute-start | bytes 1179656 | tf_op jit(solution)/shard_map/ppermute | solution.py:123
  124.7 3.0 %copy-start.5 = (f32[3,256,256]{2,1,0:T(8,128)S(1)}, f32[3,256,256]{2,1,0:T(8,128)}, u32[]{:S(2)}) copy-start(f32[3,256,256]{2,1,0:T(8,128)} %copy-done.4) | copy-start | bytes 2359300
  129.8 7.9 %collective-permute-start.25 = (f32[896,256]{1,0:T(8,128)}, f32[896,256]{1,0:T(8,128)}, u32[]{:S(2)}, u32[]{:S(2)}) collective-permute-start(f32[896,256]{1,0:T(8,128)} %dynamic-slice_bitcast_fusion), channel_id=1, source_target_pairs={{0,1},{1,0},{2,3},{3,2},{4,5},{5,4},{6,7},{7,6},{8,9},{9,8},{10,11... | collective-permute-start | bytes 2752520 | tf_op jit(solution)/shard_map/ppermute | solution.py:123
  130.2 6.5 %collective-permute-start.26 = (f32[192,256]{1,0:T(8,128)S(1)}, f32[192,256]{1,0:T(8,128)}, u32[]{:S(2)}, u32[]{:S(2)}) collective-permute-start(f32[192,256]{1,0:T(8,128)S(1)} %dynamic-slice_bitcast_fusion.4), channel_id=1, source_target_pairs={{0,2},{1,3},{2,0},{3,1},{4,6},{5,7},{6,4},{7,5},{8,10},{9,11},{10,... | collective-permute-start | bytes 589832 | tf_op jit(solution)/shard_map/ppermute | solution.py:123
  139.1 18.5 %collective-permute-start.27 = (f32[448,256]{1,0:T(8,128)S(1)}, f32[448,256]{1,0:T(8,128)S(1)}, u32[]{:S(2)}, u32[]{:S(2)}) collective-permute-start(f32[448,256]{1,0:T(8,128)S(1)} %dynamic-slice_bitcast_fusion.1), channel_id=1, source_target_pairs={{0,2},{1,3},{2,0},{3,1},{4,6},{5,7},{6,4},{7,5},{8,10},{9,11},{10,... | collective-permute-start | bytes 1376264 | tf_op jit(solution)/shard_map/ppermute | solution.py:123
  139.4 5.2 %collective-permute-start.28 = (f32[192,256]{1,0:T(8,128)S(1)}, f32[192,256]{1,0:T(8,128)S(1)}, u32[]{:S(2)}, u32[]{:S(2)}) collective-permute-start(f32[192,256]{1,0:T(8,128)S(1)} %bitcast_add_fusion.4), channel_id=1, source_target_pairs={{0,4},{1,5},{2,6},{3,7},{4,0},{5,1},{6,2},{7,3},{8,12},{9,13},{10,... | collective-permute-start | bytes 589832 | tf_op jit(solution)/shard_map/ppermute | solution.py:123
  144.5 12.2 %collective-permute-start.29 = (f32[192,256]{1,0:T(8,128)S(1)}, f32[192,256]{1,0:T(8,128)S(1)}, u32[]{:S(2)}, u32[]{:S(2)}) collective-permute-start(f32[192,256]{1,0:T(8,128)S(1)} %add.168), channel_id=1, source_target_pairs={{0,8},{1,9},{2,10},{3,11},{4,12},{5,13},{6,14},{7,15},{8,0},{9,1},... | collective-permute-start | bytes 589832 | tf_op jit(solution)/shard_map/ppermute | solution.py:123
  156.8 5.1 %collective-permute-start.31 = (f32[192,256]{1,0:T(8,128)S(1)}, f32[192,256]{1,0:T(8,128)S(1)}, u32[]{:S(2)}, u32[]{:S(2)}) collective-permute-start(f32[192,256]{1,0:T(8,128)S(1)} %add.169), channel_id=1, source_target_pairs={{0,2},{1,3},{2,0},{3,1},{4,6},{5,7},{6,4},{7,5},{8,10},{9,11},{10,... | collective-permute-start | bytes 589832 | tf_op jit(solution)/shard_map/ppermute | solution.py:123
  161.9 5.1 %collective-permute-start.32 = (f32[384,256]{1,0:T(8,128)S(1)}, f32[384,256]{1,0:T(8,128)S(1)}, u32[]{:S(2)}, u32[]{:S(2)}) collective-permute-start(f32[384,256]{1,0:T(8,128)S(1)} %bitcast.305), channel_id=1, source_target_pairs={{0,1},{1,0},{2,3},{3,2},{4,5},{5,4},{6,7},{7,6},{8,9},{9,8},{10,11... | collective-permute-start | bytes 1179656 | tf_op jit(solution)/shard_map/ppermute | solution.py:123
  164.3 8.6 %collective-permute-start.30 = (f32[224,256]{1,0:T(8,128)S(1)}, f32[224,256]{1,0:T(8,128)S(1)}, u32[]{:S(2)}, u32[]{:S(2)}) collective-permute-start(f32[224,256]{1,0:T(8,128)S(1)} %dynamic-slice_bitcast_fusion.3), channel_id=1, source_target_pairs={{0,4},{1,5},{2,6},{3,7},{4,0},{5,1},{6,2},{7,3},{8,12},{9,13},{10,... | collective-permute-start | bytes 688136 | tf_op jit(solution)/shard_map/ppermute | solution.py:123
  173.0 7.0 %collective-permute-start.33 = (f32[112,256]{1,0:T(8,128)S(1)}, f32[112,256]{1,0:T(8,128)S(1)}, u32[]{:S(2)}, u32[]{:S(2)}) collective-permute-start(f32[112,256]{1,0:T(8,128)S(1)} %dynamic-slice_bitcast_fusion.8), channel_id=1, source_target_pairs={{0,8},{1,9},{2,10},{3,11},{4,12},{5,13},{6,14},{7,15},{8,0},{9,1},... | collective-permute-start | bytes 344072 | tf_op jit(solution)/shard_map/ppermute | solution.py:123
  179.9 10.7 %copy-start.19 = (s32[512]{0:T(512)S(1)}, s32[512]{0:T(512)}, u32[]{:S(2)}) copy-start(s32[512]{0:T(512)} %param.21) | copy-start | bytes 6148
  179.9 10.7 %copy-start.22 = (s32[64]{0:T(128)S(1)}, s32[64]{0:T(128)}, u32[]{:S(2)}) copy-start(s32[64]{0:T(128)} %param.22) | copy-start | bytes 772
  180.1 8.2 %collective-permute-start.34 = (f32[112,256]{1,0:T(8,128)S(1)}, f32[112,256]{1,0:T(8,128)S(1)}, u32[]{:S(2)}, u32[]{:S(2)}) collective-permute-start(f32[112,256]{1,0:T(8,128)S(1)} %bitcast_add_fusion.5), channel_id=1, source_target_pairs={{0,8},{1,9},{2,10},{3,11},{4,12},{5,13},{6,14},{7,15},{8,0},{9,1},... | collective-permute-start | bytes 344072 | tf_op jit(solution)/shard_map/ppermute | solution.py:123
  188.4 7.8 %collective-permute-start.35 = (f32[224,256]{1,0:T(8,128)S(1)}, f32[224,256]{1,0:T(8,128)S(1)}, u32[]{:S(2)}, u32[]{:S(2)}) collective-permute-start(f32[224,256]{1,0:T(8,128)S(1)} %bitcast.309), channel_id=1, source_target_pairs={{0,4},{1,5},{2,6},{3,7},{4,0},{5,1},{6,2},{7,3},{8,12},{9,13},{10,... | collective-permute-start | bytes 688136 | tf_op jit(solution)/shard_map/ppermute | solution.py:123
  196.2 11.1 %collective-permute-start.36 = (f32[448,256]{1,0:T(8,128)S(1)}, f32[448,256]{1,0:T(8,128)S(1)}, u32[]{:S(2)}, u32[]{:S(2)}) collective-permute-start(f32[448,256]{1,0:T(8,128)S(1)} %bitcast.304), channel_id=1, source_target_pairs={{0,2},{1,3},{2,0},{3,1},{4,6},{5,7},{6,4},{7,5},{8,10},{9,11},{10,... | collective-permute-start | bytes 1376264 | tf_op jit(solution)/shard_map/ppermute | solution.py:123
  208.4 7.6 %copy-start.20 = (bf16[4,1024]{1,0:T(4,128)(2,1)S(1)}, bf16[4,1024]{1,0:T(4,128)(2,1)}, u32[]{:S(2)}) copy-start(bf16[4,1024]{1,0:T(4,128)(2,1)} %param.23) | copy-start | bytes 24580
  208.4 54.6 %all-to-all-start = ((bf16[16,4,16,1024]{3,2,1,0:T(8,128)(2,1)}), bf16[16,4,16,1024]{3,2,1,0:T(8,128)(2,1)S(1)}, u32[]{:S(2)}, u32[]{:S(2)}) async-start(bf16[16,4,16,1024]{3,2,1,0:T(8,128)(2,1)} %bitcast.300), calls=%async_computation | async-start | bytes 4194304 | tf_op jit(solution)/shard_map/all_to_all | solution.py:560
  215.7 2.7 %collective-permute-start.37 = (f32[896,256]{1,0:T(8,128)}, f32[896,256]{1,0:T(8,128)S(1)}, u32[]{:S(2)}, u32[]{:S(2)}) collective-permute-start(f32[896,256]{1,0:T(8,128)} %bitcast.299), channel_id=1, source_target_pairs={{0,1},{1,0},{2,3},{3,2},{4,5},{5,4},{6,7},{7,6},{8,9},{9,8},{10,11... | collective-permute-start | bytes 2752520 | tf_op jit(solution)/shard_map/ppermute | solution.py:123
  219.8 48.8 %copy-start.1 = (bf16[2048,64]{0,1:T(8,128)(2,1)S(1)}, bf16[2048,64]{0,1:T(8,128)(2,1)}, u32[]{:S(2)}) copy-start(bf16[2048,64]{0,1:T(8,128)(2,1)} %param.20) | copy-start | bytes 786436
  (16 other events, 24.5 us)
